TPU v7x, 128 devices: a whole 4x4x4 slice. The times are simulated.
128 devices in a mesh: expert: 4 (over z), dp: 32 (over x, y, core).
Axes of the slice: x: 4, y: 4, z: 4, core: 2. Of those that a mesh axis runs over, the one named last changes fastest.
Arguments:
- grad_terms: bfloat16 [32, 4, 7168, 1024], P('dp', None, 'expert'), may hold values from -1000 to 1000
- momentum: float32 [4, 2, 4, 1792, 1024], P('expert', None, None, 'dp'), may hold values from -6 to 6
- weights: float32 [4, 7168, 1024], P(None, ('expert', 'dp')), may hold values from -4 to 4
- owner_list: int32 [4], replicated, may hold values from 0 to 3, as said below
Outputs:
- new_weights: float32 [4, 7168, 1024], P(None, ('expert', 'dp'))
- update: bfloat16 [4, 7168, 1024], P(None, ('expert', 'dp'))
- new_momentum: float32 [4, 2, 4, 1792, 1024], P('expert', None, None, 'dp')
- direction_rms: float32 [4], replicated
Inputs may be any that keep to these rules, and one draw needn't show every extreme that they name: `owner_list`: each of the 4 groups owns at most 2 of the 4 matrices, and some group owns exactly 2.
All inputs are finite; a program needn't handle non-finite values.
Results may differ from a plain program's by a relative error of at most 0.035.
Values may be sent and summed in bfloat16 or wider, within the bound.
A program may use at most 128 MiB of HBM per device.

v0:
```python
import math

import jax
import jax.numpy as jnp
from jax import lax
from jax.sharding import PartitionSpec as P

D = 7168
FF = 1024
ITERS = 3


MOMENT = 0.95
CLIP_RMS = 1.0
LEARN = 0.1
DECAY = 0.1
COEF_A = 3.4445
COEF_B = -4.775
COEF_C = 2.0315
NORM_EPS = 1e-07
MEAN_EPS = 1e-06
HIGH_PREC = lax.Precision.HIGHEST


def owner_table(owner_list, groups, slot_count):
    matrices = owner_list.shape[0]
    positions = jnp.arange(matrices)
    same_owner = owner_list[:, None] == owner_list[None, :]
    earlier = positions[None, :] < positions[:, None]
    slot_number = jnp.sum(jnp.where(same_owner & earlier, 1, 0), axis=1).astype(jnp.int32)
    by_group = owner_list[None, :] == jnp.arange(groups)[:, None]
    by_slot = slot_number[None, :] == jnp.arange(slot_count)[:, None]
    return (by_group[:, None, :] & by_slot[None, :, :]).astype(jnp.float32)


def clip_factor(total_sq, entry_count):
    return jnp.minimum(1.0, CLIP_RMS / jnp.sqrt(total_sq / entry_count + MEAN_EPS))


def per_device(grad_terms, momentum, weights, owner_list):
    groups = lax.axis_size("expert")
    my_group = lax.axis_index("expert")
    slot_count = momentum.shape[1]
    summed = lax.psum_scatter(grad_terms[0], "dp", scatter_dimension=1, tiled=True).astype(
        jnp.float32
    )
    gradient_input = summed.astype(jnp.bfloat16)
    entry_count = float(gradient_input.shape[0] * D * FF)
    assign_owner = owner_table(owner_list, groups, slot_count)
    group_mask = jnp.arange(groups) == my_group
    outgoing = jnp.einsum(
        "dlv,vpi->ldpi",
        assign_owner.astype(jnp.bfloat16),
        gradient_input,
        preferred_element_type=jnp.float32,
    ).astype(jnp.bfloat16)
    arrived = lax.all_to_all(outgoing, "expert", split_axis=1, concat_axis=1, tiled=True)
    moment_old = momentum[0]
    slot_grads = arrived.astype(jnp.float32)
    total_sq = lax.psum(jnp.sum(jnp.square(gradient_input.astype(jnp.float32))), ("expert", "dp"))
    factor = clip_factor(total_sq, entry_count)
    moment_new = MOMENT * moment_old + factor * slot_grads
    update_dir = factor * slot_grads + MOMENT * moment_new
    local_sq = jnp.sum(jnp.square(update_dir), axis=(1, 2, 3))
    placed_sq = jnp.where(group_mask[:, None], local_sq[None], 0.0)
    all_sq = lax.psum(placed_sq, ("expert", "dp"))
    squares = jnp.sum(jnp.where(group_mask[:, None], all_sq, 0.0), axis=0)
    matrix_sq = jnp.einsum("gsm,gs->m", assign_owner, all_sq, precision=HIGH_PREC)
    direction_rms = jnp.sqrt(matrix_sq / float(D * FF))
    norm_value = jnp.sqrt(squares) + NORM_EPS
    current = (update_dir / norm_value[:, None, None, None]).astype(jnp.bfloat16)
    kept_shape = current.shape
    flat_rows = current.reshape(kept_shape[0], kept_shape[1] * kept_shape[2], kept_shape[3])
    for iteration in range(ITERS):
        partial_value = jnp.einsum(
            "krf,krg->kfg", flat_rows, flat_rows, preferred_element_type=jnp.float32
        ).astype(jnp.bfloat16)
        gram_matrix = lax.psum(partial_value, "dp").astype(jnp.float32).astype(jnp.bfloat16)
        product_one = jnp.einsum(
            "krf,kfg->krg", flat_rows, gram_matrix, preferred_element_type=jnp.float32
        ).astype(jnp.bfloat16)
        product_two = jnp.einsum(
            "krf,kfg->krg", product_one, gram_matrix, preferred_element_type=jnp.float32
        )
        flat_rows = (
            COEF_A * flat_rows.astype(jnp.float32)
            + COEF_B * product_one.astype(jnp.float32)
            + COEF_C * product_two
        ).astype(jnp.bfloat16)
    result = flat_rows.reshape(kept_shape)
    returned_output = lax.all_to_all(result, "expert", split_axis=1, concat_axis=1, tiled=True)
    orthogonal = jnp.einsum(
        "qlk,lqao->kao",
        assign_owner.astype(jnp.bfloat16),
        returned_output,
        preferred_element_type=jnp.float32,
    )
    new_moment = moment_new[None]
    scale_rms = 0.2 * math.sqrt(max(D, FF))
    update = (scale_rms * orthogonal).astype(jnp.bfloat16)
    new_weights = weights * (1.0 - LEARN * DECAY) - LEARN * scale_rms * orthogonal
    return (new_weights, update, new_moment, direction_rms)


def solution(mesh):
    placed = (
        P("dp", None, "expert", None),
        P("expert", None, None, "dp", None),
        P(None, ("expert", "dp"), None),
        P(),
    )
    return jax.shard_map(
        per_device,
        mesh=mesh,
        in_specs=placed,
        out_specs=(
            P(None, ("expert", "dp"), None),
            P(None, ("expert", "dp"), None),
            P("expert", None, None, "dp", None),
            P(),
        ),
        check_vma=False,
    )
```

profile of v0, /device:TPU:1, one launch (start us, length us, event | category | flops | bytes accessed | tf_op | source)
XLA Modules:
  0.0 674.3 jit_solution(6352515510814187019)
XLA Ops:
  7.2 16.9 %copy.48 = bf16[4,1792,1024]{2,0,1:T(4,128)(2,1)S(1)} copy(bf16[4,1792,1024]{2,1,0:T(8,128)(2,1)} %bitcast.68) | data formatting | bytes 29360128
  24.1 9.5 %copy.50 = bf16[224,8,4,1024]{3,1,2,0:T(8,128)(2,1)} copy(bf16[224,8,4,1024]{3,2,1,0:T(4,128)(2,1)S(1)} %bitcast.67) | data formatting | bytes 29360128
  33.6 0.6 copy-done.5
  34.4 111.1 %reduce-scatter.4.cloned.1.call-done = bf16[56,4096]{1,0:T(8,128)(2,1)} async-done(((bf16[1792,4096]{1,0:T(8,128)(2,1)}), bf16[56,4096]{1,0:T(8,128)(2,1)}) %reduce-scatter.4.cloned.1.call-update) | async-done | bytes 458768
  145.5 1.4 reshape.73
  146.8 0.8 fusion.1
  147.6 1.2 copy.37
  148.8 4.1 all-to-all-start
  152.9 0.8 multiply_reduce_fusion.1
  153.7 67.5 %psum.35 = f32[]{:T(128)} all-reduce(f32[]{:T(128)} %multiply_reduce_fusion.1), channel_id=1, replica_groups=mesh['expert'=4,'dp'=32] {'expert','dp'}, use_global_device_ids=true, to_apply=%region_3.4 | all-reduce | flops 1 | bytes 8 | tf_op jit(solution)/shard_map/psum | solution.py:60
  222.0 0.6 multiply_reduce_fusion
  222.6 62.6 %psum.36 = f32[4,2]{0,1:T(2,128)S(1)} all-reduce(f32[4,2]{0,1:T(2,128)S(1)} %broadcast_select_fusion), channel_id=1, replica_groups=mesh['expert'=4,'dp'=32] {'expert','dp'}, use_global_device_ids=true, to_apply=%region_5.6 | all-reduce | flops 8 | bytes 64 | tf_op jit(solution)/shard_map/psum | solution.py:66
  285.4 3.3 fusion
  288.7 3.3 convolution_convert_fusion.2
  292.2 108.5 %all-reduce.4.cloned.1.call-done = bf16[2,1024,1024]{2,1,0:T(8,128)(2,1)} async-done(((bf16[2,1024,1024]{2,1,0:T(8,128)(2,1)}), bf16[2,1024,1024]{2,1,0:T(8,128)(2,1)}) %all-reduce.4.cloned.1.call-update) | async-done | bytes 4194320 | tf_op jit(solution)/shard_map/psum | solution.py:78
  400.7 3.5 convolution_convert_fusion.5
  404.2 1.4 add_convert_fusion.2
  405.6 3.3 convolution_convert_fusion.1
  408.9 111.3 %all-reduce.6.cloned.1.call-done = bf16[2,1024,1024]{2,1,0:T(8,128)(2,1)} async-done(((bf16[2,1024,1024]{2,1,0:T(8,128)(2,1)}), bf16[2,1024,1024]{2,1,0:T(8,128)(2,1)}) %all-reduce.6.cloned.1.call-update) | async-done | bytes 4194320 | tf_op jit(solution)/shard_map/psum | solution.py:78
  520.2 3.5 convolution_convert_fusion.4
  523.7 1.4 add_convert_fusion.1
  525.1 3.3 convolution_convert_fusion
  528.4 111.2 %all-reduce.8.cloned.1.call-done = bf16[2,1024,1024]{2,1,0:T(8,128)(2,1)} async-done(((bf16[2,1024,1024]{2,1,0:T(8,128)(2,1)}), bf16[2,1024,1024]{2,1,0:T(8,128)(2,1)}) %all-reduce.8.cloned.1.call-update) | async-done | bytes 4194320 | tf_op jit(solution)/shard_map/psum | solution.py:78
  639.6 3.5 convolution_convert_fusion.3
  643.1 1.4 add_convert_fusion
  644.5 1.9 copy.39
  646.4 4.1 all-to-all-start.1
  650.5 0.7 fusion.3
  651.3 12.0 %all-to-all-done.1 = bf16[2,4,56,1024]{3,0,2,1:T(2,128)(2,1)S(1)} async-done(((bf16[2,4,56,1024]{3,0,2,1:T(2,128)(2,1)}), bf16[2,4,56,1024]{3,0,2,1:T(2,128)(2,1)S(1)}, u32[]{:S(2)}, u32[]{:S(2)}) %all-to-all-start.1) | async-done | bytes 917536 | tf_op jit(solution)/shard_map/all_to_all | solution.py:91
  663.3 2.1 multiply_convert_fusion
  665.4 1.5 copy.41
  666.8 0.9 copy.42
  (27 shorter events, 0.8 us)
Async XLA Ops:
  7.2 138.3 %reduce-scatter.4.cloned.1.call-start = ((), (), s32[]{:S(2)}) async-start(), calls=%async_computation.6 | async-start | bytes 15138816
  33.5 0.7 copy-start.5
  147.6 74.4 %copy-start = (f32[1,2,4,56,1024]{4,3,2,1,0:T(8,128)S(1)}, f32[1,2,4,56,1024]{4,3,2,1,0:T(8,128)}, u32[]{:S(2)}) copy-start(f32[1,2,4,56,1024]{4,3,2,1,0:T(8,128)} %param.5) | copy-start | bytes 5505028
  148.8 73.2 %all-to-all-start = ((bf16[2,4,56,1024]{3,2,0,1:T(8,128)(2,1)}), bf16[2,4,56,1024]{3,2,0,1:T(8,128)(2,1)S(1)}, u32[]{:S(2)}, u32[]{:S(2)}) async-start(bf16[2,4,56,1024]{3,2,0,1:T(8,128)(2,1)} %copy.37), calls=%async_computation | async-start | bytes 1835008 | tf_op jit(solution)/shard_map/all_to_all | solution.py:57
  152.9 247.8 %all-reduce.4.cloned.1.call-start = ((), (), s32[]{:S(2)}) async-start(), calls=%async_computation.3 | async-start | bytes 8388608 | tf_op jit(solution)/shard_map/psum | solution.py:78
  292.0 228.2 %all-reduce.6.cloned.1.call-start = ((), (), s32[]{:S(2)}) async-start(), calls=%async_computation.4 | async-start | bytes 8388608 | tf_op jit(solution)/shard_map/psum | solution.py:78
  400.7 3.5 copy-start.1
  408.9 230.8 %all-reduce.8.cloned.1.call-start = ((), (), s32[]{:S(2)}) async-start(), calls=%async_computation.5 | async-start | bytes 8388608 | tf_op jit(solution)/shard_map/psum | solution.py:78
  520.2 3.5 copy-start.2
  639.6 3.5 copy-start.3
  644.5 18.8 %copy-start.4 = (f32[4,56,1024]{2,1,0:T(8,128)S(1)}, f32[4,56,1024]{2,1,0:T(8,128)}, u32[]{:S(2)}) copy-start(f32[4,56,1024]{2,1,0:T(8,128)} %param.6) | copy-start | bytes 2752516
  646.4 16.9 %all-to-all-start.1 = ((bf16[2,4,56,1024]{3,0,2,1:T(2,128)(2,1)}), bf16[2,4,56,1024]{3,0,2,1:T(2,128)(2,1)S(1)}, u32[]{:S(2)}, u32[]{:S(2)}) async-start(bf16[2,4,56,1024]{3,0,2,1:T(2,128)(2,1)} %copy.39), calls=%async_computation.1 | async-start | bytes 1835008 | tf_op jit(solution)/shard_map/all_to_all | solution.py:91
Sparse Core Ops, SparseCore 0:
  33.7 111.7 reduce-scatter.3
  292.1 108.5 all-reduce.3
  409.0 111.1 all-reduce.5
  528.5 111.0 all-reduce.7
where the time goes:
time: 675 us; the launch traced here: 674 us
  waiting for transfers between devices  454 us (67%)
  blocking collectives  130 us (19%)
  local copies, waits for them, and re-layouts  33.8 us (5%)
  matrix products  27.9 us (4%)
  between operations  14.6 us (2%)
  starting transfers between devices  8.54 us (1%)
    psum x3, waiting for transfers between devices, per_device(): lax.psum(partial_value, 'dp').astype(jnp.float32).astype(jnp.bfloat16)  331 us
    unnamed x5, waiting for transfers between devices  111 us
    psum x1, blocking collectives, per_device(): lax.psum(jnp.sum(jnp.square(gradient_input.astype(jnp.float32))), ('exper...  67.5 us
    psum x1, blocking collectives, per_device(): all_sq = lax.psum(placed_sq, ('expert', 'dp'))  62.6 us
    unnamed x17, local copies, waits for them, and re-layouts  30.7 us
  transfers between devices with their start and end apart: 6, of which 5 were waited for; matrix products, arithmetic and copies ran while one was open for 0% of the time, Pallas kernels for 0%

commit v1 on v0

v1 whole, which is shorter than its diff:
```python
import functools
import math

import jax
import jax.numpy as jnp
from jax import lax
from jax.experimental import pallas as pl
from jax.experimental.pallas import tpu as pltpu
from jax.sharding import PartitionSpec as P

D = 7168
FF = 1024
MATS = 4
SLOTS = 2
GROUPS = 4
SIDE = 4
BLOCK = 112
HALF = FF // 2
LANES = 128
CHUNKS = HALF // LANES
PANEL = 256
PART = 80

MOMENT = 0.95
CLIP_RMS = 1.0
LEARN = 0.1
DECAY = 0.1
COEF_A = 3.4445
COEF_B = -4.775
COEF_C = 2.0315
NORM_EPS = 1e-07
MEAN_EPS = 1e-06
F32 = jnp.float32
BF16 = jnp.bfloat16


def place():
    e = lax.axis_index("expert")
    p = lax.axis_index("dp")
    return e, p // 8, (p // 2) % 4, p % 2


def target(e, x, y, c):
    return {"expert": e, "dp": x * 8 + y * 2 + c}


def wrap(v):
    return lax.rem(v + 4, 4)


def greet(e, x, y, c):
    barrier = pltpu.get_barrier_semaphore()
    others = [target(e, wrap(x + dx), wrap(y + dy), c) for dx in range(4) for dy in range(4) if dx + dy]
    others += [target(wrap(e + dz), x, y, lax.rem(c + dc, 2)) for dz in range(4) for dc in range(2) if dz + dc]
    for other in others:
        pl.semaphore_signal(barrier, inc=1, device_id=other)
    pl.semaphore_wait(barrier, len(others))


def remote(src, dst, send, recv, device):
    return pltpu.make_async_remote_copy(src_ref=src, dst_ref=dst, send_sem=send, recv_sem=recv, device_id=device)


def lanes_sum(v):
    return jnp.sum(jnp.sum(v, axis=0, keepdims=True), axis=1, keepdims=True)


def reduce_kernel(table, g, mom, zin, mom_sib, total, own, sib, tr1, dr1, cb1, mid, tr2, dr2, cb2, res, zout,
                  acc, column, plane, own_s, sib_s, sib_r, s1, r1, s2, r2, zs, zr, zl, ms, cs, cr, ps, pr):
    e, x, y, c = place()
    other = 1 - c

    def own_copy(k, m):
        cols = pl.ds(pl.multiple_of(c * HALF + k * LANES, LANES), LANES)
        return pltpu.make_async_copy(g.at[m, :, :, :, cols], own.at[k, m], own_s.at[k, m])

    def sib_copy(k, m):
        cols = pl.ds(pl.multiple_of(other * HALF + k * LANES, LANES), LANES)
        return remote(g.at[m, :, :, :, cols], sib.at[k, m], sib_s.at[k, m], sib_r.at[k, m], target(e, x, y, other))

    for k in range(CHUNKS):
        for m in range(MATS):
            own_copy(k, m).start()
    greet(e, x, y, c)
    for k in range(CHUNKS):
        for m in range(MATS):
            sib_copy(k, m).start()
    mom_copy = remote(mom.at[other], mom_sib, ms.at[0], ms.at[1], target(e, x, y, other))
    mom_copy.start()
    acc[...] = jnp.zeros_like(acc)

    def along(m, first, step):
        on_x = (m < 2) == first
        pos = x if on_x else y
        dev = target(e, wrap(x + step), y, c) if on_x else target(e, x, wrap(y + step), c)
        return pos, dev

    def sign(m):
        return 1 if m % 2 else -1

    def group(ref, k, m, i):
        return ref.at[k, m, i] if m < 2 else ref.at[k, m, :, i]

    def copies1(k, m):
        d = sign(m)
        pos, ahead = along(m, True, d)
        _, back = along(m, True, -d)
        return (
            remote(group(own, k, m, wrap(pos + 2)), tr1.at[k, m], s1.at[k, m, 0], r1.at[k, m, 0], ahead),
            remote(group(own, k, m, wrap(pos - d)), dr1.at[k, m], s1.at[k, m, 1], r1.at[k, m, 1], back),
            remote(group(own, k, m, wrap(pos + d)), cb1.at[k, m], s1.at[k, m, 2], r1.at[k, m, 2], ahead),
        )

    def copies2(k, m):
        d = sign(m)
        pos, ahead = along(m, False, d)
        _, back = along(m, False, -d)
        return (
            remote(mid.at[k, m, wrap(pos + 2)], tr2.at[k, m], s2.at[k, m, 0], r2.at[k, m, 0], ahead),
            remote(mid.at[k, m, wrap(pos - d)], dr2.at[k, m], s2.at[k, m, 1], r2.at[k, m, 1], back),
            remote(mid.at[k, m, wrap(pos + d)], cb2.at[k, m], s2.at[k, m, 2], r2.at[k, m, 2], ahead),
        )

    def z_copy(k, dz, dc):
        j = 2 * dz + dc
        dst = zin.at[e, c, :, pl.ds(pl.multiple_of(k * LANES, LANES), LANES)]
        if j == 0:
            return pltpu.make_async_copy(zout.at[k, 0], dst, zl.at[k])
        return remote(zout.at[k, j], dst, zs.at[k, j], zr.at[k, j], target(wrap(e + dz), x, y, lax.rem(c + dc, 2)))

    def stage_a(k):
        for m in range(MATS):
            own_copy(k, m).wait()
            sib_copy(k, m).wait_recv()
            pos, _ = along(m, True, 1)
            i = wrap(pos + 2)
            to, more = group(own, k, m, i), group(sib, k, m, i)
            for j in range(SIDE):
                to[j] = (to[j].astype(F32) + more[j].astype(F32)).astype(BF16)
            copies1(k, m)[0].start()
        for m in range(MATS):
            pos, _ = along(m, True, 1)
            i = wrap(pos - sign(m))
            to, more = group(own, k, m, i), group(sib, k, m, i)
            for j in range(SIDE):
                to[j] = (to[j].astype(F32) + more[j].astype(F32)).astype(BF16)
            copies1(k, m)[1].start()

    def stage_b(k):
        for m in range(MATS):
            copies = copies1(k, m)
            copies[0].wait_recv()
            pos, _ = along(m, True, 1)
            i = wrap(pos + sign(m))
            to, more, came = group(own, k, m, i), group(sib, k, m, i), tr1.at[k, m]
            for j in range(SIDE):
                to[j] = (to[j].astype(F32) + more[j].astype(F32) + came[j].astype(F32)).astype(BF16)
            copies[2].start()

    def stage_c(k):
        for m in range(MATS):
            copies = copies1(k, m)
            copies[1].wait_recv()
            copies[2].wait_recv()
            pos, _ = along(m, True, 1)
            to, more, came, came2 = group(own, k, m, pos), group(sib, k, m, pos), dr1.at[k, m], cb1.at[k, m]
            for j in range(SIDE):
                v = (to[j].astype(F32) + more[j].astype(F32)) + (came[j].astype(F32) + came2[j].astype(F32))
                mid[k, m, j] = v.astype(BF16)
            copies = copies2(k, m)
            copies[0].start()
            copies[1].start()

    def stage_d(k):
        for m in range(MATS):
            copies = copies2(k, m)
            copies[0].wait_recv()
            pos, _ = along(m, False, 1)
            i = wrap(pos + sign(m))
            mid[k, m, i] = (mid[k, m, i].astype(F32) + tr2[k, m].astype(F32)).astype(BF16)
            copies[2].start()

    def stage_e(k):
        for m in range(MATS):
            copies = copies2(k, m)
            copies[1].wait_recv()
            copies[2].wait_recv()
            pos, _ = along(m, False, 1)
            v = mid[k, m, pos].astype(F32) + (dr2[k, m].astype(F32) + cb2[k, m].astype(F32))
            v = v.astype(BF16).astype(F32)
            res[m] = v
            acc[...] += jnp.sum(jnp.square(v).reshape(BLOCK // 8, 8, LANES), axis=0)
        for dz in (2, 1, 3, 0):
            for dc in range(2):
                slot = wrap(e + dz) * SLOTS + lax.rem(c + dc, 2)
                v = table[slot, 0] * res[0]
                for m in range(1, MATS):
                    v = v + table[slot, m] * res[m]
                zout[k, 2 * dz + dc] = v.astype(BF16)
                z_copy(k, dz, dc).start()

    stages = (stage_a, stage_b, stage_c, stage_d, stage_e)

    def step(t, carry):
        for lag, stage in enumerate(stages):
            @pl.when((t >= lag) & (t < CHUNKS + lag))
            def _():
                stage(t - lag)
        return carry

    lax.fori_loop(0, CHUNKS + len(stages) - 1, step, 0)

    me_col = 2 * e + c
    column[me_col] = acc[...]
    sums = []
    for dz in range(4):
        for dc in range(2):
            if dz + dc:
                j = 2 * dz + dc
                sums.append(remote(acc, column.at[me_col], cs.at[j], cr.at[j],
                                   target(wrap(e + dz), x, y, lax.rem(c + dc, 2))))
    for copy in sums:
        copy.start()
    for copy in sums:
        copy.wait()
    v = column[0]
    for j in range(1, 8):
        v = v + column[j]
    acc[...] = v
    me_plane = 4 * x + y
    plane[me_plane] = v
    sums = []
    for dx in range(4):
        for dy in range(4):
            if dx + dy:
                j = 4 * dx + dy
                sums.append(remote(acc, plane.at[me_plane], ps.at[j], pr.at[j],
                                   target(e, wrap(x + dx), wrap(y + dy), c)))
    for copy in sums:
        copy.start()
    for copy in sums:
        copy.wait()
    v = plane[0]
    for j in range(1, 16):
        v = v + plane[j]
    total[...] = v

    def drain(k, carry):
        for m in range(MATS):
            sib_copy(k, m).wait_send()
            for copy in copies1(k, m) + copies2(k, m):
                copy.wait_send()
        for dz in range(4):
            for dc in range(2):
                z_copy(k, dz, dc).wait()
        return carry

    lax.fori_loop(0, CHUNKS, drain, 0)
    mom_copy.wait()


def gram_kernel(zin, total, mom, mom_sib, new_mom, ret, squares, buf, X, packed, full, rs1, cb, rs1b, mid, rs2, out2, G, A,
                B, Y, back, acc, plane, sq_in, ls, ns, s1, r1, s2, r2, s3, r3, s4, r4, ps, pr, qs, qr, bs, br):
    e, x, y, c = place()
    other = 1 - c
    loads = [
        pltpu.make_async_copy(mom.at[c], buf.at[:, pl.ds(pl.multiple_of(56 * c, 8), 56)], ls.at[0]),
        pltpu.make_async_copy(mom_sib, buf.at[:, pl.ds(pl.multiple_of(56 * other, 8), 56)], ls.at[1]),
    ]
    for copy in loads:
        copy.start()
    greet(e, x, y, c)
    mean = lanes_sum(total[...]) / float(MATS * D * FF)
    factor = jnp.minimum(1.0, CLIP_RMS / jnp.sqrt(mean + MEAN_EPS))
    for copy in loads:
        copy.wait()
    acc[...] = jnp.zeros_like(acc)

    def direction(i, carry):
        for h in range(2):
            cols = pl.ds(h * HALF, HALF)
            grad = factor * zin[i, h].astype(F32)
            moved = MOMENT * buf[i, :, cols] + grad
            buf[i, :, cols] = moved
            v = grad + MOMENT * moved
            X[i, :, cols] = v.astype(BF16)
            sq = jnp.sum(jnp.square(v).reshape(BLOCK // 8, 8, HALF), axis=0)
            acc[...] += sq[:, :128] + sq[:, 128:256] + sq[:, 256:384] + sq[:, 384:]
        return carry

    lax.fori_loop(0, 4, direction, 0)
    new_copies = [
        pltpu.make_async_copy(buf.at[:, pl.ds(pl.multiple_of(56 * c, 8), 56)], new_mom.at[c], ns.at[0]),
        remote(buf.at[:, pl.ds(pl.multiple_of(56 * other, 8), 56)], new_mom.at[c], ns.at[1], ns.at[2],
               target(e, x, y, other)),
    ]
    me_plane = 4 * x + y
    plane[me_plane] = acc[...]
    sums = []
    for dx in range(4):
        for dy in range(4):
            if dx + dy:
                j = 4 * dx + dy
                sums.append(remote(acc, plane.at[me_plane], ps.at[j], pr.at[j],
                                   target(e, wrap(x + dx), wrap(y + dy), c)))
    for copy in sums:
        copy.start()

    rows = X[...].reshape(4 * BLOCK, FF)
    at = 0
    for i in range(4):
        left = rows[:, i * PANEL:(i + 1) * PANEL]
        for j in range(i, 4):
            block = lax.dot_general(left, rows[:, j * PANEL:(j + 1) * PANEL], (((0,), (0,)), ((), ())),
                                    preferred_element_type=F32).astype(BF16)
            packed[at:at + PANEL] = block[:, :LANES]
            packed[at + PANEL:at + 2 * PANEL] = block[:, LANES:]
            at += 2 * PANEL

    def sign(r):
        return 1 if r % 2 else -1

    def along(r, first, step):
        on_x = (r < 2) == first
        pos = x if on_x else y
        dev = target(e, wrap(x + step), y, c) if on_x else target(e, x, wrap(y + step), c)
        return pos, dev

    def group(ref, r, i):
        return ref.at[pl.ds(pl.multiple_of((4 * r + i) * 4 * PART, 16), 4 * PART)]

    def single(ref, r, i, j):
        return ref.at[pl.ds(pl.multiple_of((16 * r + 4 * i + j) * PART, 16), PART)]

    def first_copies(r):
        d = sign(r)
        pos, ahead = along(r, True, d)
        _, back_dev = along(r, True, -d)
        return (
            remote(group(packed, r, wrap(pos + 2)), rs1.at[r, 0], s1.at[r, 0], r1.at[r, 0], ahead),
            remote(group(packed, r, wrap(pos - d)), rs1.at[r, 1], s1.at[r, 1], r1.at[r, 1], back_dev),
            remote(cb.at[r], rs1.at[r, 2], s1.at[r, 2], r1.at[r, 2], ahead),
        )

    def second_copies(r):
        pos, _ = along(r, False, 1)
        out = []
        for step in (2, 1, 3):
            _, dev = along(r, False, step)
            src = mid.at[r, pl.ds(pl.multiple_of(wrap(pos + step) * PART, 16), PART)]
            out.append(remote(src, rs2.at[r, step - 1], s2.at[r, step - 1], r2.at[r, step - 1], dev))
        return out

    def third_copies(r):
        pos1, _ = along(r, True, 1)
        pos2, _ = along(r, False, 1)
        out = []
        for step in (2, 1, 3):
            _, dev = along(r, False, step)
            out.append(remote(out2.at[r], single(full, r, pos1, pos2), s3.at[r, step - 1], r3.at[r, step - 1], dev))
        return out

    def fourth_copies(r):
        d = sign(r)
        pos, ahead = along(r, True, d)
        _, back_dev = along(r, True, -d)
        own = group(full, r, pos)
        passed = group(full, r, wrap(pos - d))
        return (
            remote(own, own, s4.at[r, 0], r4.at[r, 0], ahead),
            remote(own, own, s4.at[r, 1], r4.at[r, 1], back_dev),
            remote(passed, passed, s4.at[r, 2], r4.at[r, 2], ahead),
        )

    ROUTES = (0, 2, 1, 3)
    for r in ROUTES:
        copies = first_copies(r)
        copies[0].start()
        copies[1].start()
    for copy in new_copies:
        copy.start()
    for r in ROUTES:
        copies = first_copies(r)
        copies[0].wait_recv()
        pos, _ = along(r, True, 1)
        mine = group(packed, r, wrap(pos + sign(r)))
        cb[r] = (mine[...].astype(F32) + rs1[r, 0].astype(F32)).astype(BF16)
        copies[2].start()
    for r in ROUTES:
        copies = first_copies(r)
        copies[1].wait_recv()
        copies[2].wait_recv()
        pos, _ = along(r, True, 1)
        mine = group(packed, r, pos)
        mid[r] = (mine[...].astype(F32) + (rs1[r, 1].astype(F32) + rs1[r, 2].astype(F32))).astype(BF16)
        for copy in second_copies(r):
            copy.start()
    for r in ROUTES:
        for copy in second_copies(r):
            copy.wait_recv()
        pos, _ = along(r, False, 1)
        v = mid[r, pl.ds(pl.multiple_of(pos * PART, 16), PART)].astype(F32) + rs2[r, 0].astype(F32)
        v = v + (rs2[r, 1].astype(F32) + rs2[r, 2].astype(F32))
        out2[r] = v.astype(BF16)
    for r in ROUTES:
        pos1, _ = along(r, True, 1)
        pos2, _ = along(r, False, 1)
        single(full, r, pos1, pos2)[...] = out2[r]
        for copy in third_copies(r):
            copy.start()
    for copy in sums:
        copy.wait()
    v = plane[0]
    for j in range(1, 16):
        v = v + plane[j]
    acc[...] = v
    sq_copies = []
    for dz in range(4):
        for dc in range(2):
            if dz + dc:
                j = 2 * dz + dc
                sq_copies.append(remote(acc, sq_in.at[2 * e + c], qs.at[j], qr.at[j],
                                        target(wrap(e + dz), x, y, lax.rem(c + dc, 2))))
    sq_in[2 * e + c] = v
    for copy in sq_copies:
        copy.start()
    norm = jnp.sqrt(lanes_sum(v)) + NORM_EPS
    inv = 1.0 / norm
    inv2 = inv * inv
    for r in ROUTES:
        for copy in third_copies(r):
            copy.wait_recv()
        copies = fourth_copies(r)
        copies[0].start()
        copies[1].start()
    for r in ROUTES:
        copies = fourth_copies(r)
        copies[0].wait_recv()
        copies[2].start()
    for r in ROUTES:
        copies = fourth_copies(r)
        copies[1].wait_recv()
        copies[2].wait_recv()

    at = 0
    for i in range(4):
        for j in range(i, 4):
            for h in range(2):
                block = full[at:at + PANEL]
                G[i * PANEL:(i + 1) * PANEL, j * PANEL + h * LANES:j * PANEL + (h + 1) * LANES] = block
                if i != j:
                    G[j * PANEL + h * LANES:j * PANEL + (h + 1) * LANES, i * PANEL:(i + 1) * PANEL] = block.T
                at += PANEL

    def product(lhs, rhs, out, finish):
        def body(i, carry):
            rows_i = pl.ds(pl.multiple_of(i * PANEL, PANEL), PANEL)
            for j in range(2):
                cols = pl.ds(j * HALF, HALF)
                v = jnp.dot(lhs[rows_i], rhs[:, cols], preferred_element_type=F32)
                out[rows_i, cols] = finish(v, rows_i, cols).astype(BF16)
            return carry
        lax.fori_loop(0, 4, body, 0)

    def advance(rhs, scale):
        for i in range(4):
            v = X[i]
            X[i] = (scale * (COEF_A * v.astype(F32) + jnp.dot(v, rhs[...], preferred_element_type=F32))).astype(BF16)

    def polynomial(src, q, t, out, scale):
        b_s = COEF_B * scale
        c_s = COEF_C * scale * scale
        product(src, src, q, lambda v, i, j: b_s * src[i, j].astype(F32) + c_s * v)
        product(src, q, t, lambda v, i, j: scale * (COEF_A * src[i, j].astype(F32) + v))
        product(t, q, out, lambda v, i, j: COEF_A * t[i, j].astype(F32) + v)

    polynomial(G, A, B, G, inv2)
    advance(A, inv)
    polynomial(G, A, B, G, 1.0)
    advance(A, 1.0)

    def finish(i, carry):
        v = X[i]
        w = jnp.dot(v, G[...], preferred_element_type=F32).astype(BF16)
        z = jnp.dot(w, G[...], preferred_element_type=F32)
        out = COEF_A * v.astype(F32) + COEF_B * w.astype(F32) + COEF_C * z
        Y[...] = out
        for h in range(2):
            for k in range(2):
                back[i, h, k * 56:(k + 1) * 56] = Y[h * 56:(h + 1) * 56, k * HALF:(k + 1) * HALF].astype(BF16)
        return carry

    lax.fori_loop(0, 4, finish, 0)
    returns = []
    for dz in (2, 1, 3, 0):
        for dc in range(2):
            j = 2 * dz + dc
            src = back.at[wrap(e + dz), lax.rem(c + dc, 2)]
            dst = ret.at[e, c]
            if j == 0:
                returns.append(pltpu.make_async_copy(src, dst, bs.at[0]))
            else:
                returns.append(remote(src, dst, bs.at[j], br.at[j], target(wrap(e + dz), x, y, lax.rem(c + dc, 2))))
    for copy in returns:
        copy.start()
    for copy in sq_copies:
        copy.wait()
    squares[...] = sq_in[...]
    for r in ROUTES:
        for copy in second_copies(r) + third_copies(r):
            copy.wait_send()
        for copy in first_copies(r):
            copy.wait_send()
        for copy in fourth_copies(r):
            copy.wait_send()
    for copy in new_copies:
        copy.wait()
    for copy in returns:
        copy.wait()


def assignment(owner_list):
    positions = jnp.arange(MATS)
    same_owner = owner_list[:, None] == owner_list[None, :]
    earlier = positions[None, :] < positions[:, None]
    slot_number = jnp.sum(jnp.where(same_owner & earlier, 1, 0), axis=1).astype(jnp.int32)
    place_of = owner_list * SLOTS + slot_number
    return place_of, (place_of[None, :] == jnp.arange(GROUPS * SLOTS)[:, None]).astype(F32)


ANY = pl.BlockSpec(memory_space=pl.ANY)
VMEM = pl.BlockSpec(memory_space=pltpu.VMEM)
SMEM = pl.BlockSpec(memory_space=pltpu.SMEM)
DMA = pltpu.SemaphoreType.DMA


def per_device(grad_terms, momentum, weights, owner_list):
    place_of, table = assignment(owner_list)
    mom = momentum[0]
    small = (CHUNKS, MATS, BLOCK, LANES)
    large = (CHUNKS, MATS, SIDE, BLOCK, LANES)
    whole = (CHUNKS, MATS, SIDE, SIDE, BLOCK, LANES)
    zin, mom_sib, total = pl.pallas_call(
        reduce_kernel,
        name="reduce_terms",
        out_shape=(
            jax.ShapeDtypeStruct((GROUPS, 2, BLOCK, HALF), BF16),
            jax.ShapeDtypeStruct((GROUPS, 56, FF), F32),
            jax.ShapeDtypeStruct((8, LANES), F32),
        ),
        in_specs=[SMEM, ANY, ANY],
        out_specs=(ANY, ANY, VMEM),
        scratch_shapes=[
            pltpu.VMEM(whole, BF16), pltpu.VMEM(whole, BF16),
            pltpu.VMEM(large, BF16), pltpu.VMEM(large, BF16), pltpu.VMEM(large, BF16), pltpu.VMEM(large, BF16),
            pltpu.VMEM(small, BF16), pltpu.VMEM(small, BF16), pltpu.VMEM(small, BF16),
            pltpu.VMEM((MATS, BLOCK, LANES), F32),
            pltpu.VMEM((CHUNKS, 8, BLOCK, LANES), BF16),
            pltpu.VMEM((8, LANES), F32), pltpu.VMEM((8, 8, LANES), F32), pltpu.VMEM((16, 8, LANES), F32),
            DMA((CHUNKS, MATS)), DMA((CHUNKS, MATS)), DMA((CHUNKS, MATS)),
            DMA((CHUNKS, MATS, 3)), DMA((CHUNKS, MATS, 3)), DMA((CHUNKS, MATS, 3)), DMA((CHUNKS, MATS, 3)),
            DMA((CHUNKS, 8)), DMA((CHUNKS, 8)), DMA((CHUNKS,)), DMA((2,)),
            DMA((8,)), DMA((8,)), DMA((16,)), DMA((16,)),
        ],
        compiler_params=pltpu.CompilerParams(collective_id=0, has_side_effects=True, vmem_limit_bytes=56 << 20),
    )(table, grad_terms.reshape(MATS, SIDE, SIDE, BLOCK, FF), mom)

    new_mom, ret, squares = pl.pallas_call(
        gram_kernel,
        name="orthogonalize",
        out_shape=(
            jax.ShapeDtypeStruct((SLOTS, GROUPS, 56, FF), F32),
            jax.ShapeDtypeStruct((GROUPS, SLOTS, BLOCK, HALF), BF16),
            jax.ShapeDtypeStruct((GROUPS * SLOTS, 8, LANES), F32),
        ),
        in_specs=[VMEM, VMEM, ANY, ANY],
        out_specs=(ANY, ANY, VMEM),
        scratch_shapes=[
            pltpu.VMEM((GROUPS, BLOCK, FF), F32),
            pltpu.VMEM((GROUPS, BLOCK, FF), BF16),
            pltpu.VMEM((64 * PART, LANES), BF16), pltpu.VMEM((64 * PART, LANES), BF16),
            pltpu.VMEM((4, 3, 4 * PART, LANES), BF16),
            pltpu.VMEM((4, 4 * PART, LANES), BF16),
            pltpu.VMEM((8, LANES), F32),
            pltpu.VMEM((4, 4 * PART, LANES), BF16),
            pltpu.VMEM((4, 3, PART, LANES), BF16),
            pltpu.VMEM((4, PART, LANES), BF16),
            pltpu.VMEM((FF, FF), BF16), pltpu.VMEM((FF, FF), BF16), pltpu.VMEM((FF, FF), BF16),
            pltpu.VMEM((BLOCK, FF), F32),
            pltpu.VMEM((GROUPS, 2, BLOCK, HALF), BF16),
            pltpu.VMEM((8, LANES), F32), pltpu.VMEM((16, 8, LANES), F32), pltpu.VMEM((8, 8, LANES), F32),
            DMA((2,)), DMA((3,)),
            DMA((4, 3)), DMA((4, 3)), DMA((4, 3)), DMA((4, 3)), DMA((4, 3)), DMA((4, 3)), DMA((4, 3)), DMA((4, 3)),
            DMA((16,)), DMA((16,)), DMA((8,)), DMA((8,)), DMA((8,)), DMA((8,)),
        ],
        compiler_params=pltpu.CompilerParams(collective_id=1, has_side_effects=True, vmem_limit_bytes=56 << 20),
    )(zin, total, mom, mom_sib)

    rows = ret.reshape(GROUPS * SLOTS, 2, 56, HALF)[place_of]
    rows = rows.transpose(0, 2, 1, 3).reshape(MATS, 56, FF).astype(F32)
    direction_rms = jnp.sqrt(jnp.sum(squares, axis=(1, 2))[place_of] / float(D * FF))
    scale_rms = 0.2 * math.sqrt(max(D, FF))
    update = (scale_rms * rows).astype(BF16)
    new_weights = weights * (1.0 - LEARN * DECAY) - LEARN * scale_rms * rows
    return (new_weights, update, new_mom[None], direction_rms)


def solution(mesh):
    placed = (
        P("dp", None, "expert", None),
        P("expert", None, None, "dp", None),
        P(None, ("expert", "dp"), None),
        P(),
    )
    return jax.shard_map(
        per_device,
        mesh=mesh,
        in_specs=placed,
        out_specs=(
            P(None, ("expert", "dp"), None),
            P(None, ("expert", "dp"), None),
            P("expert", None, None, "dp", None),
            P(),
        ),
        check_vma=False,
    )
```

time: 675 us -> 149 us (0.22)
  waiting for transfers between devices: 454 us -> 0 us
  Pallas kernels: 0 us -> 138 us
  blocking collectives: 130 us -> 0 us
  local copies, waits for them, and re-layouts: 33.8 us -> 5.03 us
  matrix products: 27.9 us -> 0 us
  between operations: 14.6 us -> 0.69 us
  starting transfers between devices: 8.54 us -> 0 us
    psum x3 -> x0, waiting for transfers between devices: 331 us -> none  [per_device(): lax.psum(partial_value, 'dp').astype(jnp.float32).astype(jnp.bfloat16)]
    pallas_call x0 -> x2, Pallas kernels: none -> 138 us  [the longest x1 70 us: per_device(): pl.pallas_call(reduce_kernel, name='reduce_terms', out_shape=(jax.ShapeDt...]
    psum x2 -> x0, blocking collectives: 130 us -> none  [the longest x1 67.5 us: per_device(): lax.psum(jnp.sum(jnp.square(gradient_input.astype(jnp.float32))), ('exper...]
    unnamed x5 -> x0, waiting for transfers between devices: 111 us -> none
    unnamed x17 -> x5, local copies, waits for them, and re-layouts: 30.7 us -> 1.74 us
    dot_general x12 -> x0, matrix products: 27.9 us -> none  [the longest x3 10.4 us: per_device(): jnp.einsum('krf,kfg->krg', flat_rows, gram_matrix, preferred_element_type...]
    all_to_all x2 -> x0, waiting for transfers between devices: 12 us -> none  [the longest x1 12 us: per_device(): lax.all_to_all(result, 'expert', split_axis=1, concat_axis=1, tiled=True)]
    all_to_all x2 -> x0, starting transfers between devices: 8.23 us -> none  [the longest x1 4.14 us: per_device(): lax.all_to_all(result, 'expert', split_axis=1, concat_axis=1, tiled=True)]
  transfers between devices with their start and end apart: 6 -> 0, of which waited for: 5 -> 0; matrix products, arithmetic and copies ran while one was open for 0% -> 0% of each run, Pallas kernels for 0% -> 0%
where the time goes in v1:
time: 149 us
  Pallas kernels  138 us (93%)
  local copies, waits for them, and re-layouts  5.03 us (3%)
  other arithmetic  4.81 us (3%)
    pallas_call x1, Pallas kernels, per_device(): pl.pallas_call(reduce_kernel, name='reduce_terms', out_shape=(jax.ShapeDt...  70 us
    pallas_call x1, Pallas kernels, per_device(): pl.pallas_call(gram_kernel, name='orthogonalize', out_shape=(jax.ShapeDty...  68.1 us

profile of v1, /device:TPU:1, one launch (start us, length us, event | category | flops | bytes accessed | tf_op | source)
XLA Modules:
  0.0 148.6 jit_solution(4835615562867451213)
XLA Ops:
  0.6 0.9 select_reduce_fusion
  1.5 0.7 compare_select_fusion
  2.2 0.6 fusion.3.table
  2.8 70.0 %reduce_terms.1 = (bf16[4,2,112,512]{3,2,1,0:T(8,128)(2,1)}, f32[4,56,1024]{2,1,0:T(8,128)}, f32[8,128]{1,0:T(8,128)}) custom-call(f32[8,4]{1,0:T(8,128)} %fusion.3.table, bf16[4,4,4,112,1024]{4,3,2,1,0:T(8,128)(2,1)} %bitcast.12, f32[2,4,56,1024]{3,2,1,0:T(8,128)} %bitcast.13), custom_call_target="tpu_custom_call" | custom-call | tf_op jit(solution)/shard_map/reduce_terms/pallas_call | solution.py:543
  72.8 68.1 %orthogonalize.1 = (f32[2,4,56,1024]{3,2,1,0:T(8,128)}, bf16[4,2,112,512]{3,2,1,0:T(8,128)(2,1)}, f32[8,8,128]{2,1,0:T(8,128)}) custom-call(bf16[4,2,112,512]{3,2,1,0:T(8,128)(2,1)} %get-tuple-element.10.zin, f32[8,128]{1,0:T(8,128)} %get-tuple-element.11.total, f32[2,4,56,1024]{3,2,1,0:T(8,128)} %bitcast.14, f32[4,56,1024]{2,1,0:T(8,128)} %get-tuple-element.12.mom_sib), custom_call_target="tpu_custom_call" | custom-call | tf_op jit(solution)/shard_map/orthogonalize/pallas_call | solution.py:568
  140.9 1.8 %gather_fusion = bf16[4,2,56,512]{3,2,1,0:T(8,128)(2,1)S(1)} fusion(bf16[8,2,56,512]{3,2,1,0:T(8,128)(2,1)} %bitcast.18, s32[1024]{0:T(1024)S(1)} %pad_clamp_fusion), kind=kCustom, calls=%fused_computation | custom fusion | bytes 917520 | tf_op jit(solution)/shard_map/gather | solution.py:599
  142.6 0.9 reduce_sum.19
  143.5 0.6 gather_fusion.1
  144.2 0.5 multiply_sqrt_fusion
  144.7 0.2 fusion.2
  144.8 0.0 copy-start.1
  144.9 0.8 copy.15
  145.7 0.1 copy.14
  145.8 0.0 copy-start
  145.8 0.4 copy-done.1
  146.2 1.1 multiply_subtract_fusion
  147.2 0.1 copy-done
  147.3 1.2 copy.17
  (1 shorter events, 0.0 us)
Async XLA Ops:
  144.8 1.3 copy-start.1
  145.8 1.6 %copy-start = (f32[2,4,56,1024]{3,2,1,0:T(8,128)S(1)}, f32[2,4,56,1024]{3,2,1,0:T(8,128)}, u32[]{:S(2)}) copy-start(f32[2,4,56,1024]{3,2,1,0:T(8,128)} %get-tuple-element.14) | copy-start | bytes 5505028

commit v2 on v0

v2 whole, which is shorter than its diff:
```python
import math

import jax
import jax.numpy as jnp
from jax import lax
from jax.experimental import pallas as pl
from jax.experimental.pallas import tpu as pltpu
from jax.sharding import PartitionSpec as P

D = 7168
FF = 1024
MATS = 4
SLOTS = 2
GROUPS = 4
SIDE = 4
BLOCK = 112
ROWS = 56
HALF = FF // 2
LANES = 128
CHUNKS = HALF // LANES
LAST = CHUNKS - 1
PANEL = 256
PART = 80

MOMENT = 0.95
CLIP_RMS = 1.0
LEARN = 0.1
DECAY = 0.1
COEF_A = 3.4445
COEF_B = -4.775
COEF_C = 2.0315
NORM_EPS = 1e-07
MEAN_EPS = 1e-06
F32 = jnp.float32
BF16 = jnp.bfloat16

COLUMN = ((2, 0), (2, 1), (1, 0), (1, 1), (3, 0), (3, 1), (0, 1))
PLANE = tuple((dx, dy) for dx in range(4) for dy in range(4) if dx + dy)


def wrap(v):
    return lax.rem(v + 4, 4)


def remote(src, dst, send, recv, device):
    return pltpu.make_async_remote_copy(src_ref=src, dst_ref=dst, send_sem=send, recv_sem=recv, device_id=device)


def whole_sum(v):
    return jnp.sum(jnp.sum(v, axis=0, keepdims=True), axis=1, keepdims=True)


def sign(m):
    return 1 if m % 2 else -1


def muon_kernel(owners, g, mom, new_mom, rows_out, rms_out,
                own, sib, tr1, dr1, cb1, mid, tr2, dr2, cb2, res, zout, zin, buf, X, packed, full, rs1, cbg, midg, rs2,
                out2, G, A, B, T, X2, back, ret, acc, acc2, acc3, acc4, column, plane, plane2, sq_in,
                own_s, sib_s, sib_r, s1, r1, s2, r2, zs, zr, zl, ms, cs, cr, ps, pr, ns, g1s, g1r, g2s, g2r, g3s, g3r,
                g4s, g4r, ps2, pr2, qs, qr, bs, br):
    e = lax.axis_index("expert")
    p = lax.axis_index("dp")
    x, y, c = p // 8, (p // 2) % 4, p % 2
    other = 1 - c

    def target(te, tx, ty, tc):
        return {"expert": te, "dp": tx * 8 + ty * 2 + tc}

    def in_column(dz, dc):
        return target(wrap(e + dz), x, y, lax.rem(c + dc, 2))

    def in_plane(dx, dy):
        return target(e, wrap(x + dx), wrap(y + dy), c)

    places = []
    for m in range(MATS):
        number = jnp.int32(0)
        for m2 in range(m):
            number = number + jnp.where(owners[m2] == owners[m], 1, 0)
        places.append(owners[m] * SLOTS + number)

    def mask(m, slot):
        return jnp.where(places[m] == slot, 1.0, 0.0).astype(F32)

    def own_copy(k, m):
        cols = pl.ds(pl.multiple_of(c * HALF + k * LANES, LANES), LANES)
        return pltpu.make_async_copy(g.at[m, :, :, :, cols], own.at[k, m], own_s.at[k, m])

    def sib_copy(k, m):
        cols = pl.ds(pl.multiple_of(other * HALF + k * LANES, LANES), LANES)
        return remote(g.at[m, :, :, :, cols], sib.at[k, m], sib_s.at[k, m], sib_r.at[k, m], in_column(0, 1))

    def along(m, first, step):
        on_x = (m < 2) == first
        return (x, in_plane(step, 0)) if on_x else (y, in_plane(0, step))

    def group(ref, k, m, i):
        return ref.at[k, m, i] if m < 2 else ref.at[k, m, :, i]

    def copy1(k, m, which):
        d = sign(m)
        pos, dev = along(m, True, -d if which == 1 else d)
        i = wrap(pos + (2, -d, d)[which])
        return remote(group(own, k, m, i), (tr1, dr1, cb1)[which].at[k, m], s1.at[k, m, which], r1.at[k, m, which], dev)

    def copy2(k, m, which):
        d = sign(m)
        pos, dev = along(m, False, -d if which == 1 else d)
        i = wrap(pos + (2, -d, d)[which])
        return remote(mid.at[k, m, i], (tr2, dr2, cb2)[which].at[k, m], s2.at[k, m, which], r2.at[k, m, which], dev)

    def copy2_last(m, which):
        step = (2, 1, 3)[which]
        pos, dev = along(m, False, step)
        return remote(mid.at[LAST, m, wrap(pos + step)], (tr2, dr2, cb2)[which].at[LAST, m], s2.at[LAST, m, which],
                      r2.at[LAST, m, which], dev)

    def z_copy(k, dz, dc):
        j = 2 * dz + dc
        dst = zin.at[e, c, :, pl.ds(pl.multiple_of(k * LANES, LANES), LANES)]
        if j == 0:
            return pltpu.make_async_copy(zout.at[k, 0], dst, zl.at[k])
        return remote(zout.at[k, j], dst, zs.at[k, j], zr.at[k, j], in_column(dz, dc))

    mine_rows = pl.ds(pl.multiple_of(ROWS * c, 8), ROWS)
    other_rows = pl.ds(pl.multiple_of(ROWS * other, 8), ROWS)
    mom_own = pltpu.make_async_copy(mom.at[c], buf.at[:, mine_rows], ms.at[0])
    mom_sib = remote(mom.at[other], buf.at[:, mine_rows], ms.at[1], ms.at[2], in_column(0, 1))

    for k in range(CHUNKS):
        for m in range(MATS):
            own_copy(k, m).start()
    mom_own.start()
    barrier = pltpu.get_barrier_semaphore()
    for dz, dc in COLUMN:
        pl.semaphore_signal(barrier, inc=1, device_id=in_column(dz, dc))
    for dx, dy in PLANE:
        pl.semaphore_signal(barrier, inc=1, device_id=in_plane(dx, dy))
    pl.semaphore_wait(barrier, len(COLUMN) + len(PLANE))
    for k in range(CHUNKS):
        for m in range(MATS):
            sib_copy(k, m).start()
    mom_sib.start()
    acc[...] = jnp.zeros_like(acc)
    acc3[...] = jnp.zeros_like(acc3)

    def pair_sum(k, m, i):
        to, more = group(own, k, m, i), group(sib, k, m, i)
        for j in range(SIDE):
            to[j] = (to[j].astype(F32) + more[j].astype(F32)).astype(BF16)

    def transit(k):
        for m in range(MATS):
            own_copy(k, m).wait()
            sib_copy(k, m).wait_recv()
            pos, _ = along(m, True, 1)
            pair_sum(k, m, wrap(pos + 2))
            copy1(k, m, 0).start()

    def combine(k):
        for m in range(MATS):
            copy1(k, m, 0).wait_recv()
            pos, _ = along(m, True, 1)
            i = wrap(pos + sign(m))
            to, more, came = group(own, k, m, i), group(sib, k, m, i), tr1.at[k, m]
            for j in range(SIDE):
                to[j] = (to[j].astype(F32) + more[j].astype(F32) + came[j].astype(F32)).astype(BF16)
            copy1(k, m, 2).start()

    def direct(k):
        for m in range(MATS):
            pos, _ = along(m, True, 1)
            pair_sum(k, m, wrap(pos - sign(m)))
            copy1(k, m, 1).start()

    def turn(k):
        for m in range(MATS):
            copy1(k, m, 1).wait_recv()
            copy1(k, m, 2).wait_recv()
            pos, _ = along(m, True, 1)
            to, more, came, came2 = group(own, k, m, pos), group(sib, k, m, pos), dr1.at[k, m], cb1.at[k, m]
            for j in range(SIDE):
                v = (to[j].astype(F32) + more[j].astype(F32)) + (came[j].astype(F32) + came2[j].astype(F32))
                mid[k, m, j] = v.astype(BF16)

            @pl.when(k < LAST)
            def _():
                copy2(k, m, 0).start()
                copy2(k, m, 1).start()

            @pl.when(k == LAST)
            def _():
                for which in range(3):
                    copy2_last(m, which).start()

    def combine2(k):
        for m in range(MATS):
            copy2(k, m, 0).wait_recv()
            pos, _ = along(m, False, 1)
            i = wrap(pos + sign(m))
            mid[k, m, i] = (mid[k, m, i].astype(F32) + tr2[k, m].astype(F32)).astype(BF16)
            copy2(k, m, 2).start()

    def collect(k, m, v):
        v = v.astype(BF16).astype(F32)
        res[m] = v
        acc[...] += jnp.sum(jnp.square(v).reshape(BLOCK // 8, 8, LANES), axis=0)

    def send_slots(k):
        for dz in (2, 1, 3, 0):
            for dc in range(2):
                slot = wrap(e + dz) * SLOTS + lax.rem(c + dc, 2)
                v = mask(0, slot) * res[0]
                for m in range(1, MATS):
                    v = v + mask(m, slot) * res[m]
                zout[k, 2 * dz + dc] = v.astype(BF16)
                z_copy(k, dz, dc).start()

    def finish_sum(k):
        for m in range(MATS):
            copy2(k, m, 1).wait_recv()
            copy2(k, m, 2).wait_recv()
            pos, _ = along(m, False, 1)
            collect(k, m, mid[k, m, pos].astype(F32) + (dr2[k, m].astype(F32) + cb2[k, m].astype(F32)))
        send_slots(k)

    stages = ((transit, 0, CHUNKS), (combine, 1, CHUNKS), (direct, 2, CHUNKS), (turn, 3, CHUNKS),
              (combine2, 4, LAST), (finish_sum, 5, LAST))

    def step(t, carry):
        for stage, lag, chunks in stages:
            @pl.when((t >= lag) & (t < chunks + lag))
            def _():
                stage(t - lag)
        return carry

    lax.fori_loop(0, LAST + 5, step, 0)
    for m in range(MATS):
        for which in range(3):
            copy2_last(m, which).wait_recv()
        pos, _ = along(m, False, 1)
        v = mid[LAST, m, pos].astype(F32) + tr2[LAST, m].astype(F32)
        collect(LAST, m, v + (dr2[LAST, m].astype(F32) + cb2[LAST, m].astype(F32)))

    me_column = 2 * e + c
    me_plane = 4 * x + y

    def spread_column(src, dst, send, recv):
        copies = [remote(src, dst.at[me_column], send.at[i], recv.at[i], in_column(*d)) for i, d in enumerate(COLUMN)]
        for copy in copies:
            copy.start()
        dst[me_column] = src[...]
        return copies

    def spread_plane(src, dst, send, recv):
        copies = [remote(src, dst.at[me_plane], send.at[i], recv.at[i], in_plane(*d)) for i, d in enumerate(PLANE)]
        for copy in copies:
            copy.start()
        dst[me_plane] = src[...]
        return copies

    def total_of(copies, ref, count):
        for copy in copies:
            copy.wait_recv()
        v = ref[0]
        for j in range(1, count):
            v = v + ref[j]
        return v

    first = spread_column(acc, column, cs, cr)
    send_slots(LAST)
    acc2[...] = total_of(first, column, 8)
    second = spread_plane(acc2, plane, ps, pr)
    mom_own.wait()
    mom_sib.wait_recv()
    for k in range(CHUNKS):
        for dz in range(4):
            for dc in range(2):
                if dz + dc:
                    z_copy(k, dz, dc).wait_recv()
                else:
                    z_copy(k, 0, 0).wait()
    mean = whole_sum(total_of(second, plane, 16)) / float(MATS * D * FF)
    factor = jnp.minimum(1.0, CLIP_RMS / jnp.sqrt(mean + MEAN_EPS))

    def direction(i, carry):
        for h in range(2):
            cols = pl.ds(h * HALF, HALF)
            grad = factor * zin[i, h].astype(F32)
            moved = MOMENT * buf[i, :, cols] + grad
            buf[i, :, cols] = moved
            v = grad + MOMENT * moved
            X[i, :, cols] = v.astype(BF16)
            sq = jnp.sum(jnp.square(v).reshape(BLOCK // 8, 8, HALF), axis=0)
            acc3[...] += sq[:, :128] + sq[:, 128:256] + sq[:, 256:384] + sq[:, 384:]
        return carry

    lax.fori_loop(0, GROUPS, direction, 0)
    new_own = pltpu.make_async_copy(buf.at[:, mine_rows], new_mom.at[c], ns.at[0])
    new_sib = remote(buf.at[:, other_rows], new_mom.at[c], ns.at[1], ns.at[2], in_column(0, 1))

    def part4(ref, r, i):
        return ref.at[pl.ds(pl.multiple_of((4 * r + i) * 4 * PART, 16), 4 * PART)]

    def part1(ref, r, i, j):
        return ref.at[pl.ds(pl.multiple_of((16 * r + 4 * i + j) * PART, 16), PART)]

    def first_copy(r, which):
        d = sign(r)
        pos, dev = along(r, True, -d if which == 1 else d)
        src = cbg.at[r] if which == 2 else part4(packed, r, wrap(pos + (2, -d)[which]))
        return remote(src, rs1.at[r, which], g1s.at[r, which], g1r.at[r, which], dev)

    def second_copy(r, step):
        pos, dev = along(r, False, step)
        src = midg.at[r, pl.ds(pl.multiple_of(wrap(pos + step) * PART, 16), PART)]
        return remote(src, rs2.at[r, step - 1], g2s.at[r, step - 1], g2r.at[r, step - 1], dev)

    def third_copy(r, step):
        pos1, _ = along(r, True, 1)
        pos2, dev = along(r, False, step)
        return remote(out2.at[r], part1(full, r, pos1, pos2), g3s.at[r, step - 1], g3r.at[r, step - 1], dev)

    def fourth_copy(r, which):
        d = sign(r)
        pos, dev = along(r, True, -d if which == 1 else d)
        ref = part4(full, r, wrap(pos - d) if which == 2 else pos)
        return remote(ref, ref, g4s.at[r, which], g4r.at[r, which], dev)

    ROUTES = (0, 1, 2, 3)
    STEPS = (2, 1, 3)
    flat = X[...].reshape(GROUPS * BLOCK, FF)
    at = 0
    for i in range(4):
        left = flat[:, i * PANEL:(i + 1) * PANEL]
        panel = lax.dot_general(left, flat[:, i * PANEL:], (((0,), (0,)), ((), ())),
                                preferred_element_type=F32).astype(BF16)
        for j in range(2 * (4 - i)):
            packed[at:at + PANEL] = panel[:, j * LANES:(j + 1) * LANES]
            at += PANEL
        first_copy(i, 0).start()
        first_copy(i, 1).start()
    squares = spread_plane(acc3, plane2, ps2, pr2)
    new_own.start()
    new_sib.start()
    for r in ROUTES:
        first_copy(r, 0).wait_recv()
        pos, _ = along(r, True, 1)
        mine = part4(packed, r, wrap(pos + sign(r)))
        cbg[r] = (mine[...].astype(F32) + rs1[r, 0].astype(F32)).astype(BF16)
        first_copy(r, 2).start()
    for r in ROUTES:
        first_copy(r, 1).wait_recv()
        first_copy(r, 2).wait_recv()
        pos, _ = along(r, True, 1)
        mine = part4(packed, r, pos)
        midg[r] = (mine[...].astype(F32) + (rs1[r, 1].astype(F32) + rs1[r, 2].astype(F32))).astype(BF16)
        for s in STEPS:
            second_copy(r, s).start()
    for r in ROUTES:
        for s in STEPS:
            second_copy(r, s).wait_recv()
        pos1, _ = along(r, True, 1)
        pos2, _ = along(r, False, 1)
        v = midg[r, pl.ds(pl.multiple_of(pos2 * PART, 16), PART)].astype(F32) + rs2[r, 0].astype(F32)
        v = (v + (rs2[r, 1].astype(F32) + rs2[r, 2].astype(F32))).astype(BF16)
        out2[r] = v
        for s in STEPS:
            third_copy(r, s).start()
        part1(full, r, pos1, pos2)[...] = v
    acc4[...] = total_of(squares, plane2, 16)
    spread = spread_column(acc4, sq_in, qs, qr)
    inv = 1.0 / (jnp.sqrt(whole_sum(acc4[...])) + NORM_EPS)
    for r in ROUTES:
        for s in STEPS:
            third_copy(r, s).wait_recv()
        fourth_copy(r, 0).start()
        fourth_copy(r, 1).start()
    for r in ROUTES:
        fourth_copy(r, 0).wait_recv()
        fourth_copy(r, 2).start()
    for r in ROUTES:
        fourth_copy(r, 1).wait_recv()
        fourth_copy(r, 2).wait_recv()
    at = 0
    for i in range(4):
        for j in range(2 * i, 8):
            block = full[at:at + PANEL]
            G[i * PANEL:(i + 1) * PANEL, j * LANES:(j + 1) * LANES] = block
            if j >= 2 * (i + 1):
                G[j * LANES:(j + 1) * LANES, i * PANEL:(i + 1) * PANEL] = block.T
            at += PANEL

    def product(lhs, rhs, out, finish):
        for i in range(4):
            low, high = i * PANEL, (i + 1) * PANEL
            v = jnp.dot(lhs[low:high], rhs[:, low:], preferred_element_type=F32)
            v = finish(v, slice(low, high), slice(low, FF)).astype(BF16)
            out[low:high, low:] = v
            for j in range(i + 1, 4):
                out[j * PANEL:(j + 1) * PANEL, low:high] = v[:, (j - i) * PANEL:(j - i + 1) * PANEL].T

    def polynomial(src, q, t, out, scale):
        b_s = COEF_B * scale
        c_s = COEF_C * scale * scale
        product(src, src, q, lambda v, i, j: b_s * src[i, j].astype(F32) + c_s * v)
        product(src, q, t, lambda v, i, j: scale * (COEF_A * src[i, j].astype(F32) + v))
        product(t, q, out, lambda v, i, j: COEF_A * t[i, j].astype(F32) + v)

    def advance(src, rhs, scale, dst):
        v = src[...].reshape(GROUPS * BLOCK, FF)
        w = scale * (COEF_A * v.astype(F32) + jnp.dot(v, rhs[...], preferred_element_type=F32))
        dst[...] = w.astype(BF16).reshape(GROUPS, BLOCK, FF)

    polynomial(G, A, B, T, inv * inv)
    advance(X, A, inv, X2)
    polynomial(T, A, B, G, 1.0)
    advance(X2, A, 1.0, X)

    def return_copy(dz, dc):
        j = 2 * dz + dc
        src = back.at[wrap(e + dz), lax.rem(c + dc, 2)]
        if j == 0:
            return pltpu.make_async_copy(src, ret.at[e, c], bs.at[0])
        return remote(src, ret.at[e, c], bs.at[j], br.at[j], in_column(dz, dc))

    for pair in ((2, 1), (3, 0)):
        v = jnp.concatenate([X[wrap(e + dz)] for dz in pair], axis=0)
        w = jnp.dot(v, G[...], preferred_element_type=F32).astype(BF16)
        z = jnp.dot(w, G[...], preferred_element_type=F32)
        z = (COEF_A * v.astype(F32) + COEF_B * w.astype(F32) + COEF_C * z).astype(BF16)
        for n, dz in enumerate(pair):
            for h in range(2):
                for k in range(2):
                    top = n * BLOCK + h * ROWS
                    back[wrap(e + dz), h, k * ROWS:(k + 1) * ROWS] = z[top:top + ROWS, k * HALF:(k + 1) * HALF]
            for dc in range(2):
                return_copy(dz, dc).start()

    for copy in spread:
        copy.wait_recv()
    lane = lax.broadcasted_iota(jnp.int32, (8, LANES), 1)
    mean_sq = jnp.zeros((8, LANES), F32)
    for slot in range(GROUPS * SLOTS):
        v = whole_sum(sq_in[slot]) / float(D * FF)
        for m in range(MATS):
            mean_sq = mean_sq + jnp.where(lane == m, mask(m, slot) * v, 0.0)
    rms_out[...] = jnp.sqrt(mean_sq)
    for k in range(CHUNKS):
        for m in range(MATS):
            sib_copy(k, m).wait_send()
            for which in range(3):
                copy1(k, m, which).wait_send()
                if k < LAST:
                    copy2(k, m, which).wait_send()
                else:
                    copy2_last(m, which).wait_send()
        for dz, dc in COLUMN:
            z_copy(k, dz, dc).wait_send()
    for r in ROUTES:
        for which in range(3):
            first_copy(r, which).wait_send()
            second_copy(r, which + 1).wait_send()
            third_copy(r, which + 1).wait_send()
            fourth_copy(r, which).wait_send()
    for copy in first + second + squares + spread:
        copy.wait_send()
    mom_sib.wait_send()
    new_own.wait()
    new_sib.wait()
    return_copy(0, 0).wait()
    for dz, dc in COLUMN:
        return_copy(dz, dc).wait()
    for m in range(MATS):
        v = mask(m, 0) * ret[0, 0].astype(F32)
        for slot in range(1, GROUPS * SLOTS):
            v = v + mask(m, slot) * ret[slot // SLOTS, slot % SLOTS].astype(F32)
        rows_out[m, :, :HALF] = v[:ROWS].astype(BF16)
        rows_out[m, :, HALF:] = v[ROWS:].astype(BF16)


ANY = pl.BlockSpec(memory_space=pl.ANY)
VMEM = pl.BlockSpec(memory_space=pltpu.VMEM)
SMEM = pl.BlockSpec(memory_space=pltpu.SMEM)
DMA = pltpu.SemaphoreType.DMA


def per_device(grad_terms, momentum, weights, owner_list):
    small = (CHUNKS, MATS, BLOCK, LANES)
    large = (CHUNKS, MATS, SIDE, BLOCK, LANES)
    whole = (CHUNKS, MATS, SIDE, SIDE, BLOCK, LANES)
    tile = pltpu.VMEM((8, LANES), F32)
    square = pltpu.VMEM((FF, FF), BF16)
    new_mom, rows, rms = pl.pallas_call(
        muon_kernel,
        name="muon",
        out_shape=(
            jax.ShapeDtypeStruct((SLOTS, GROUPS, ROWS, FF), F32),
            jax.ShapeDtypeStruct((MATS, ROWS, FF), BF16),
            jax.ShapeDtypeStruct((8, LANES), F32),
        ),
        in_specs=[SMEM, ANY, ANY],
        out_specs=(ANY, VMEM, VMEM),
        scratch_shapes=[
            pltpu.VMEM(whole, BF16), pltpu.VMEM(whole, BF16),
            pltpu.VMEM(large, BF16), pltpu.VMEM(large, BF16), pltpu.VMEM(large, BF16), pltpu.VMEM(large, BF16),
            pltpu.VMEM(small, BF16), pltpu.VMEM(small, BF16), pltpu.VMEM(small, BF16),
            pltpu.VMEM((MATS, BLOCK, LANES), F32),
            pltpu.VMEM((CHUNKS, 8, BLOCK, LANES), BF16),
            pltpu.VMEM((GROUPS, 2, BLOCK, HALF), BF16),
            pltpu.VMEM((GROUPS, BLOCK, FF), F32),
            pltpu.VMEM((GROUPS, BLOCK, FF), BF16),
            pltpu.VMEM((64 * PART, LANES), BF16), pltpu.VMEM((64 * PART, LANES), BF16),
            pltpu.VMEM((4, 3, 4 * PART, LANES), BF16),
            pltpu.VMEM((4, 4 * PART, LANES), BF16),
            pltpu.VMEM((4, 4 * PART, LANES), BF16),
            pltpu.VMEM((4, 3, PART, LANES), BF16),
            pltpu.VMEM((4, PART, LANES), BF16),
            square, square, square, square,
            pltpu.VMEM((GROUPS, BLOCK, FF), BF16),
            pltpu.VMEM((GROUPS, 2, BLOCK, HALF), BF16), pltpu.VMEM((GROUPS, SLOTS, BLOCK, HALF), BF16),
            tile, tile, tile, tile,
            pltpu.VMEM((8, 8, LANES), F32), pltpu.VMEM((16, 8, LANES), F32), pltpu.VMEM((16, 8, LANES), F32),
            pltpu.VMEM((8, 8, LANES), F32),
            DMA((CHUNKS, MATS)), DMA((CHUNKS, MATS)), DMA((CHUNKS, MATS)),
            DMA((CHUNKS, MATS, 3)), DMA((CHUNKS, MATS, 3)), DMA((CHUNKS, MATS, 3)), DMA((CHUNKS, MATS, 3)),
            DMA((CHUNKS, 8)), DMA((CHUNKS, 8)), DMA((CHUNKS,)), DMA((3,)),
            DMA((7,)), DMA((7,)), DMA((15,)), DMA((15,)), DMA((3,)),
            DMA((4, 3)), DMA((4, 3)), DMA((4, 3)), DMA((4, 3)), DMA((4, 3)), DMA((4, 3)), DMA((4, 3)), DMA((4, 3)),
            DMA((15,)), DMA((15,)), DMA((7,)), DMA((7,)), DMA((8,)), DMA((8,)),
        ],
        compiler_params=pltpu.CompilerParams(collective_id=0, has_side_effects=True, vmem_limit_bytes=60 << 20),
    )(owner_list, grad_terms.reshape(MATS, SIDE, SIDE, BLOCK, FF), momentum[0])

    rows = rows.astype(F32)
    scale_rms = 0.2 * math.sqrt(max(D, FF))
    update = (scale_rms * rows).astype(BF16)
    new_weights = weights * (1.0 - LEARN * DECAY) - LEARN * scale_rms * rows
    return (new_weights, update, new_mom[None], rms[0, :MATS])


def solution(mesh):
    placed = (
        P("dp", None, "expert", None),
        P("expert", None, None, "dp", None),
        P(None, ("expert", "dp"), None),
        P(),
    )
    return jax.shard_map(
        per_device,
        mesh=mesh,
        in_specs=placed,
        out_specs=(
            P(None, ("expert", "dp"), None),
            P(None, ("expert", "dp"), None),
            P("expert", None, None, "dp", None),
            P(),
        ),
        check_vma=False,
    )
```

time: 675 us -> 123 us (0.18)
  waiting for transfers between devices: 454 us -> 0 us
  blocking collectives: 130 us -> 0 us
  Pallas kernels: 0 us -> 118 us
  local copies, waits for them, and re-layouts: 33.8 us -> 2.56 us
  matrix products: 27.9 us -> 0 us
  between operations: 14.6 us -> 0.66 us
  starting transfers between devices: 8.54 us -> 0 us
    psum x3 -> x0, waiting for transfers between devices: 331 us -> none  [per_device(): lax.psum(partial_value, 'dp').astype(jnp.float32).astype(jnp.bfloat16)]
    psum x2 -> x0, blocking collectives: 130 us -> none  [the longest x1 67.5 us: per_device(): lax.psum(jnp.sum(jnp.square(gradient_input.astype(jnp.float32))), ('exper...]
    pallas_call x0 -> x1, Pallas kernels: none -> 118 us  [per_device(): pl.pallas_call(muon_kernel, name='muon', out_shape=(jax.ShapeDtypeStruct(...]
    unnamed x5 -> x0, waiting for transfers between devices: 111 us -> none
    unnamed x17 -> x5, local copies, waits for them, and re-layouts: 30.7 us -> 1.24 us
    dot_general x12 -> x0, matrix products: 27.9 us -> none  [the longest x3 10.4 us: per_device(): jnp.einsum('krf,kfg->krg', flat_rows, gram_matrix, preferred_element_type...]
    all_to_all x2 -> x0, waiting for transfers between devices: 12 us -> none  [the longest x1 12 us: per_device(): lax.all_to_all(result, 'expert', split_axis=1, concat_axis=1, tiled=True)]
    all_to_all x2 -> x0, starting transfers between devices: 8.23 us -> none  [the longest x1 4.14 us: per_device(): lax.all_to_all(result, 'expert', split_axis=1, concat_axis=1, tiled=True)]
  transfers between devices with their start and end apart: 6 -> 0, of which waited for: 5 -> 0; matrix products, arithmetic and copies ran while one was open for 0% -> 0% of each run, Pallas kernels for 0% -> 0%
where the time goes in v2:
time: 123 us
  Pallas kernels  118 us (96%)
  local copies, waits for them, and re-layouts  2.56 us (2%)
  other arithmetic  2.31 us (2%)
    pallas_call x1, Pallas kernels, per_device(): pl.pallas_call(muon_kernel, name='muon', out_shape=(jax.ShapeDtypeStruct(...  118 us

profile of v2, /device:TPU:1, one launch (start us, length us, event | category | flops | bytes accessed | tf_op | source)
XLA Modules:
  0.0 123.3 jit_solution(17360883853335217932)
XLA Ops:
  0.6 0.0 copy-start.1
  0.6 117.8 %muon.1 = (f32[2,4,56,1024]{3,2,1,0:T(8,128)}, bf16[4,56,1024]{2,1,0:T(8,128)(2,1)}, f32[8,128]{1,0:T(8,128)}) custom-call(s32[4]{0:T(128)} %owners.1, bf16[4,4,4,112,1024]{4,3,2,1,0:T(8,128)(2,1)} %bitcast.5, f32[2,4,56,1024]{3,2,1,0:T(8,128)} %bitcast.6), custom_call_target="tpu_custom_call" | custom-call | tf_op jit(solution)/shard_map/muon/pallas_call | solution.py:495
  118.4 0.0 copy-start
  118.4 1.3 %slice_bitcast_fusion = f32[4]{0:T(128)} fusion(f32[8,128]{1,0:T(8,128)} %get-tuple-element.9), kind=kLoop, calls=%fused_computation.4 | loop fusion | bytes 32 | tf_op jit(solution)/shard_map/squeeze | solution.py:540
  119.7 0.0 copy-done.1
  119.7 2.3 %fusion.1 = (bf16[4,56,1024]{2,1,0:T(8,128)(2,1)}, f32[4,56,1024]{2,1,0:T(8,128)}) fusion(bf16[4,56,1024]{2,1,0:T(8,128)(2,1)} %get-tuple-element.7, f32[4,56,1024]{2,1,0:T(8,128)S(1)} %copy-done.1), kind=kLoop, calls=%fused_computation.3 | loop fusion | flops 1376256 | bytes 2752512 | tf_op jit(solution)/shard_map/convert_element_type | solution.py:538
  122.1 0.0 copy-done
  122.1 1.2 copy.9
Async XLA Ops:
  0.6 119.1 %copy-start.1 = (f32[4,56,1024]{2,1,0:T(8,128)S(1)}, f32[4,56,1024]{2,1,0:T(8,128)}, u32[]{:S(2)}) copy-start(f32[4,56,1024]{2,1,0:T(8,128)} %param.6) | copy-start | bytes 2752516
  118.4 3.7 %copy-start = (f32[2,4,56,1024]{3,2,1,0:T(8,128)S(1)}, f32[2,4,56,1024]{3,2,1,0:T(8,128)}, u32[]{:S(2)}) copy-start(f32[2,4,56,1024]{3,2,1,0:T(8,128)} %get-tuple-element.8) | copy-start | bytes 5505028

commit v3 on v2

v3 whole, which is shorter than its diff:
```python
import math

import jax
import jax.numpy as jnp
from jax import lax
from jax.experimental import pallas as pl
from jax.experimental.pallas import tpu as pltpu
from jax.sharding import PartitionSpec as P

D = 7168
FF = 1024
MATS = 4
SLOTS = 2
GROUPS = 4
SIDE = 4
BLOCK = 112
ROWS = 56
HALF = FF // 2
LANES = 128
STRIP = 16
CHUNKS = BLOCK // STRIP
LAST = CHUNKS - 1
PANEL = 256
PART = 80

MOMENT = 0.95
CLIP_RMS = 1.0
LEARN = 0.1
DECAY = 0.1
COEF_A = 3.4445
COEF_B = -4.775
COEF_C = 2.0315
NORM_EPS = 1e-07
MEAN_EPS = 1e-06
F32 = jnp.float32
BF16 = jnp.bfloat16

COLUMN = ((2, 0), (2, 1), (1, 0), (1, 1), (3, 0), (3, 1), (0, 1))
PLANE = tuple((dx, dy) for dx in range(4) for dy in range(4) if dx + dy)


def wrap(v):
    return lax.rem(v + 4, 4)


def remote(src, dst, send, recv, device):
    return pltpu.make_async_remote_copy(src_ref=src, dst_ref=dst, send_sem=send, recv_sem=recv, device_id=device)


def whole_sum(v):
    return jnp.sum(jnp.sum(v, axis=0, keepdims=True), axis=1, keepdims=True)


def sign(m):
    return 1 if m % 2 else -1


def muon_kernel(owners, g, mom, new_mom, rows_out, rms_out,
                own, sib, tr1, dr1, cb1, mid, tr2, dr2, cb2, grad, zin, zout, zin2, momv, mout, min_, mall, buf, X, Xc, X2,
                packed, full, rs1, cbg, midg, rs2, out2, G, A, B, T, back, ret, acc, acc2, acc3, acc4,
                column, plane, plane2, sq_in,
                own_s, sib_s, sib_r, s1, r1, s2, r2, zs, zr, zl, ms, m1s, m1r, m2s, cs, cr, ps, pr, ns, g1s, g1r, g2s,
                g2r, g3s, g3r, g4s, g4r, g5s, g5r, ps2, pr2, qs, qr, z2s, z2r, bs, br, bl):
    e = lax.axis_index("expert")
    p = lax.axis_index("dp")
    x, y, c = p // 8, (p // 2) % 4, p % 2
    other = 1 - c

    def target(te, tx, ty, tc):
        return {"expert": te, "dp": tx * 8 + ty * 2 + tc}

    def in_column(dz, dc):
        return target(wrap(e + dz), x, y, lax.rem(c + dc, 2))

    def in_plane(dx, dy):
        return target(e, wrap(x + dx), wrap(y + dy), c)

    places = []
    for m in range(MATS):
        number = jnp.int32(0)
        for m2 in range(m):
            number = number + jnp.where(owners[m2] == owners[m], 1, 0)
        places.append(owners[m] * SLOTS + number)

    def mask(m, slot):
        return jnp.where(places[m] == slot, 1.0, 0.0).astype(F32)

    def strip(k):
        return pl.ds(pl.multiple_of(k * STRIP, STRIP), STRIP)

    def own_copy(k, m):
        cols = pl.ds(pl.multiple_of(c * HALF, HALF), HALF)
        return pltpu.make_async_copy(g.at[m, :, :, strip(k), cols], own.at[m, :, :, strip(k)], own_s.at[k, m])

    def sib_copy(k, m):
        cols = pl.ds(pl.multiple_of(other * HALF, HALF), HALF)
        return remote(g.at[m, :, :, strip(k), cols], sib.at[m, :, :, strip(k)], sib_s.at[k, m], sib_r.at[k, m],
                      in_column(0, 1))

    def along(m, first, step):
        on_x = (m < 2) == first
        return (x, in_plane(step, 0)) if on_x else (y, in_plane(0, step))

    def group(ref, k, m, i):
        return ref.at[m, i, :, strip(k)] if m < 2 else ref.at[m, :, i, strip(k)]

    def copy1(k, m, which):
        d = sign(m)
        pos, dev = along(m, True, -d if which == 1 else d)
        i = wrap(pos + (2, -d, d)[which])
        return remote(group(own, k, m, i), (tr1, dr1, cb1)[which].at[k, m], s1.at[k, m, which], r1.at[k, m, which], dev)

    def copy2(k, m, which):
        d = sign(m)
        pos, dev = along(m, False, -d if which == 1 else d)
        i = wrap(pos + (2, -d, d)[which])
        return remote(mid.at[k, m, i], (tr2, dr2, cb2)[which].at[k, m], s2.at[k, m, which], r2.at[k, m, which], dev)

    def copy2_last(m, which):
        step = (2, 1, 3)[which]
        pos, dev = along(m, False, step)
        return remote(mid.at[LAST, m, wrap(pos + step)], (tr2, dr2, cb2)[which].at[LAST, m], s2.at[LAST, m, which],
                      r2.at[LAST, m, which], dev)

    def z_copy(k, dz, dc):
        j = 2 * dz + dc
        src, dst = grad.at[wrap(e + dz), strip(k)], zin.at[e, c, strip(k)]
        if j == 0:
            return pltpu.make_async_copy(src, dst, zl.at[k])
        return remote(src, dst, zs.at[k, j], zr.at[k, j], in_column(dz, dc))

    mine_rows = pl.ds(pl.multiple_of(ROWS * c, 8), ROWS)
    other_rows = pl.ds(pl.multiple_of(ROWS * other, 8), ROWS)
    mom_load = pltpu.make_async_copy(mom, momv, ms.at[0])
    mom_own = pltpu.make_async_copy(mom.at[c], buf.at[:, mine_rows], ms.at[1])
    mom_sib = remote(mom.at[other], buf.at[:, mine_rows], ms.at[2], ms.at[3], in_column(0, 1))

    def mom_copy(dz):
        return remote(mout.at[dz], min_.at[e], m1s.at[dz], m1r.at[dz], in_column(dz, 0))

    mom_pass = remote(mall.at[c], mall.at[c], m2s.at[0], m2s.at[1], in_column(0, 1))

    for k in range(CHUNKS):
        for m in range(MATS):
            own_copy(k, m).start()
        if k == 0:
            mom_load.start()
    mom_own.start()
    barrier = pltpu.get_barrier_semaphore()
    for dz, dc in COLUMN:
        pl.semaphore_signal(barrier, inc=1, device_id=in_column(dz, dc))
    for dx, dy in PLANE:
        pl.semaphore_signal(barrier, inc=1, device_id=in_plane(dx, dy))
    pl.semaphore_wait(barrier, len(COLUMN) + len(PLANE))
    for k in range(CHUNKS):
        for m in range(MATS):
            sib_copy(k, m).start()
    acc[...] = jnp.zeros_like(acc)
    acc3[...] = jnp.zeros_like(acc3)

    def pair_sum(k, m, i):
        to, more = group(own, k, m, i), group(sib, k, m, i)
        for j in range(SIDE):
            to[j] = (to[j].astype(F32) + more[j].astype(F32)).astype(BF16)

    def transit(k):
        for m in range(MATS):
            own_copy(k, m).wait()
            sib_copy(k, m).wait_recv()
            pos, _ = along(m, True, 1)
            pair_sum(k, m, wrap(pos + 2))
            copy1(k, m, 0).start()

    def combine(k):
        for m in range(MATS):
            copy1(k, m, 0).wait_recv()
            pos, _ = along(m, True, 1)
            i = wrap(pos + sign(m))
            to, more, came = group(own, k, m, i), group(sib, k, m, i), tr1.at[k, m]
            for j in range(SIDE):
                to[j] = (to[j].astype(F32) + more[j].astype(F32) + came[j].astype(F32)).astype(BF16)
            copy1(k, m, 2).start()

    def direct(k):
        for m in range(MATS):
            pos, _ = along(m, True, 1)
            pair_sum(k, m, wrap(pos - sign(m)))
            copy1(k, m, 1).start()

    def turn(k):
        for m in range(MATS):
            copy1(k, m, 1).wait_recv()
            copy1(k, m, 2).wait_recv()
            pos, _ = along(m, True, 1)
            to, more, came, came2 = group(own, k, m, pos), group(sib, k, m, pos), dr1.at[k, m], cb1.at[k, m]
            for j in range(SIDE):
                v = (to[j].astype(F32) + more[j].astype(F32)) + (came[j].astype(F32) + came2[j].astype(F32))
                mid[k, m, j] = v.astype(BF16)

            @pl.when(k < LAST)
            def _():
                copy2(k, m, 0).start()
                copy2(k, m, 1).start()

            @pl.when(k == LAST)
            def _():
                for which in range(3):
                    copy2_last(m, which).start()

    def combine2(k):
        for m in range(MATS):
            copy2(k, m, 0).wait_recv()
            pos, _ = along(m, False, 1)
            i = wrap(pos + sign(m))
            mid[k, m, i] = (mid[k, m, i].astype(F32) + tr2[k, m].astype(F32)).astype(BF16)
            copy2(k, m, 2).start()

    def collect(k, m, v):
        v = v.astype(BF16)
        grad[m, strip(k)] = v
        v = jnp.square(v.astype(F32))
        v = v[:8] + v[8:]
        acc[...] += v[:, :128] + v[:, 128:256] + v[:, 256:384] + v[:, 384:]

    def send_strips(k):
        for dz in (2, 1, 3, 0):
            for dc in range(2):
                z_copy(k, dz, dc).start()

    def finish_sum(k):
        for m in range(MATS):
            copy2(k, m, 1).wait_recv()
            copy2(k, m, 2).wait_recv()
            pos, _ = along(m, False, 1)
            collect(k, m, mid[k, m, pos].astype(F32) + (dr2[k, m].astype(F32) + cb2[k, m].astype(F32)))
        send_strips(k)

    def mom_send(k):
        mom_load.wait()
        for dz in (2, 1, 3, 0):
            t = wrap(e + dz)
            first_is = jnp.float32(0)
            second_is = jnp.float32(0)
            for m in range(MATS):
                here = jnp.where(t == m, 1.0, 0.0).astype(F32)
                first_is = first_is + here * mask(m, 2 * e)
                second_is = second_is + here * mask(m, 2 * e + 1)
            for i in range(GROUPS):
                for h in range(2):
                    cols = slice(h * HALF, (h + 1) * HALF)
                    v = first_is * momv[0, i, :, cols] + second_is * momv[1, i, :, cols]
                    mout[dz, i, h * ROWS:(h + 1) * ROWS] = v.astype(BF16)
            if dz:
                mom_copy(dz).start()
        mom_sib.start()

    def mom_sum(k):
        for dz in (1, 2, 3):
            mom_copy(dz).wait_recv()
        for i in range(GROUPS):
            v = mout[0, i].astype(F32)
            for dz in (1, 2, 3):
                v = v + min_[wrap(e + dz), i].astype(F32)
            mall[c, i] = v.astype(BF16)
        mom_pass.start()

    stages = ((transit, 0, CHUNKS), (combine, 1, CHUNKS), (direct, 2, CHUNKS), (turn, 3, CHUNKS),
              (combine2, 4, LAST), (finish_sum, 5, LAST), (mom_send, 1, 1), (mom_sum, LAST + 2, 1))

    def step(t, carry):
        for stage, lag, chunks in stages:
            @pl.when((t >= lag) & (t < chunks + lag))
            def _():
                stage(t - lag)
        return carry

    lax.fori_loop(0, LAST + 5, step, 0)
    for m in range(MATS):
        for which in range(3):
            copy2_last(m, which).wait_recv()
        pos, _ = along(m, False, 1)
        v = mid[LAST, m, pos].astype(F32) + tr2[LAST, m].astype(F32)
        collect(LAST, m, v + (dr2[LAST, m].astype(F32) + cb2[LAST, m].astype(F32)))

    me_column = 2 * e + c
    me_plane = 4 * x + y

    def spread_column(src, dst, send, recv):
        copies = [remote(src, dst.at[me_column], send.at[i], recv.at[i], in_column(*d)) for i, d in enumerate(COLUMN)]
        for copy in copies:
            copy.start()
        dst[me_column] = src[...]
        return copies

    def spread_plane(src, dst, send, recv):
        copies = [remote(src, dst.at[me_plane], send.at[i], recv.at[i], in_plane(*d)) for i, d in enumerate(PLANE)]
        for copy in copies:
            copy.start()
        dst[me_plane] = src[...]
        return copies

    def total_of(copies, ref, count):
        for copy in copies:
            copy.wait_recv()
        v = ref[0]
        for j in range(1, count):
            v = v + ref[j]
        return v

    first = spread_column(acc, column, cs, cr)
    send_strips(LAST)
    acc2[...] = total_of(first, column, 8)
    second = spread_plane(acc2, plane, ps, pr)
    mom_pass.wait_recv()
    for k in range(CHUNKS):
        for dz in range(4):
            for dc in range(2):
                if dz + dc:
                    z_copy(k, dz, dc).wait_recv()
                else:
                    z_copy(k, 0, 0).wait()
    mean = whole_sum(total_of(second, plane, 16)) / float(MATS * D * FF)
    factor = jnp.minimum(1.0, CLIP_RMS / jnp.sqrt(mean + MEAN_EPS))

    def direction(i, carry):
        parts = [mall[k, i].astype(F32) for k in range(2)]
        for h in range(2):
            kept = jnp.concatenate([v[h * ROWS:(h + 1) * ROWS] for v in parts], axis=0)
            v = factor * zin[i, h].astype(F32)
            v = v + MOMENT * (MOMENT * kept + v)
            X[i, :, h * HALF:(h + 1) * HALF] = v.astype(BF16)
            sq = jnp.sum(jnp.square(v).reshape(BLOCK // 8, 8, HALF), axis=0)
            acc3[...] += sq[:, :128] + sq[:, 128:256] + sq[:, 256:384] + sq[:, 384:]
        return carry

    lax.fori_loop(0, GROUPS, direction, 0)

    d = 2 * c - 1

    def part4(ref, q, i):
        return ref.at[pl.ds(pl.multiple_of((4 * q + i) * 4 * PART, 16), 4 * PART)]

    def part1(ref, q, i, j):
        return ref.at[pl.ds(pl.multiple_of((16 * q + 4 * i + j) * PART, 16), PART)]

    def on(q, first, step):
        return (x, in_plane(step, 0)) if (q == 0) == first else (y, in_plane(0, step))

    def first_copy(q, which):
        pos, dev = on(q, True, -d if which == 1 else d)
        src = cbg.at[q] if which == 2 else part4(packed, q, wrap(pos + (2, -d)[which]))
        return remote(src, rs1.at[q, which], g1s.at[q, which], g1r.at[q, which], dev)

    def second_copy(q, step):
        pos, dev = on(q, False, step)
        src = midg.at[q, pl.ds(pl.multiple_of(wrap(pos + step) * PART, 16), PART)]
        return remote(src, rs2.at[q, step - 1], g2s.at[q, step - 1], g2r.at[q, step - 1], dev)

    def third_copy(q, step):
        pos1, _ = on(q, True, 1)
        pos2, dev = on(q, False, step)
        return remote(out2.at[q], part1(full.at[c], q, pos1, pos2), g3s.at[q, step - 1], g3r.at[q, step - 1], dev)

    def fourth_copy(q, which):
        pos, dev = on(q, True, -d if which == 1 else d)
        ref = part4(full.at[c], q, wrap(pos - d) if which == 2 else pos)
        return remote(ref, ref, g4s.at[q, which], g4r.at[q, which], dev)

    def pair_copy(q, n):
        pos, _ = on(q, True, 1)
        ref = part4(full.at[c], q, wrap(pos + n))
        return remote(ref, ref, g5s.at[q, n], g5r.at[q, n], in_column(0, 1))

    STEPS = (2, 1, 3)
    for j in range(4):
        cols = pl.ds(pl.multiple_of((2 * j + c) * LANES, LANES), LANES)
        Xc[:, j * LANES:(j + 1) * LANES] = X[:, :, cols].reshape(GROUPS * BLOCK, LANES)
    at = 0
    for i in range(4):
        left = X[:, :, i * PANEL:(i + 1) * PANEL].reshape(GROUPS * BLOCK, PANEL)
        panel = lax.dot_general(left, Xc[:, i * LANES:], (((0,), (0,)), ((), ())),
                                preferred_element_type=F32).astype(BF16)
        for j in range(4 - i):
            packed[at:at + PANEL] = panel[:, j * LANES:(j + 1) * LANES]
            at += PANEL
        if i in (1, 3):
            first_copy(i // 2, 0).start()
            first_copy(i // 2, 1).start()
    squares = spread_plane(acc3, plane2, ps2, pr2)
    mom_own.wait()
    mom_sib.wait_recv()
    for q in range(2):
        first_copy(q, 0).wait_recv()
        pos, _ = on(q, True, 1)
        mine = part4(packed, q, wrap(pos + d))
        cbg[q] = (mine[...].astype(F32) + rs1[q, 0].astype(F32)).astype(BF16)
        first_copy(q, 2).start()

    def slot_copy(dz, dc):
        j = 2 * dz + dc
        if j == 0:
            return pltpu.make_async_copy(zout.at[0], zin2.at[e, c], z2s.at[0])
        return remote(zout.at[j], zin2.at[e, c], z2s.at[j], z2r.at[j], in_column(dz, dc))

    for dz in (2, 1, 3, 0):
        for dc in range(2):
            slot = wrap(e + dz) * SLOTS + lax.rem(c + dc, 2)
            v = mask(0, slot) * grad[0].astype(F32)
            for m in range(1, MATS):
                v = v + mask(m, slot) * grad[m].astype(F32)
            zout[2 * dz + dc] = v.astype(BF16)
            slot_copy(dz, dc).start()

    for q in range(2):
        first_copy(q, 1).wait_recv()
        first_copy(q, 2).wait_recv()
        pos, _ = on(q, True, 1)
        mine = part4(packed, q, pos)
        midg[q] = (mine[...].astype(F32) + (rs1[q, 1].astype(F32) + rs1[q, 2].astype(F32))).astype(BF16)
        for s in STEPS:
            second_copy(q, s).start()
    for q in range(2):
        for s in STEPS:
            second_copy(q, s).wait_recv()
        pos1, _ = on(q, True, 1)
        pos2, _ = on(q, False, 1)
        v = midg[q, pl.ds(pl.multiple_of(pos2 * PART, 16), PART)].astype(F32) + rs2[q, 0].astype(F32)
        v = (v + (rs2[q, 1].astype(F32) + rs2[q, 2].astype(F32))).astype(BF16)
        out2[q] = v
        for s in STEPS:
            third_copy(q, s).start()
        part1(full.at[c], q, pos1, pos2)[...] = v
    acc4[...] = total_of(squares, plane2, 16)
    spread = spread_column(acc4, sq_in, qs, qr)
    inv = 1.0 / (jnp.sqrt(whole_sum(acc4[...])) + NORM_EPS)
    for q in range(2):
        for s in STEPS:
            third_copy(q, s).wait_recv()
        fourth_copy(q, 0).start()
        fourth_copy(q, 1).start()
        pair_copy(q, 0).start()
    for q in range(2):
        fourth_copy(q, 0).wait_recv()
        fourth_copy(q, 2).start()
    for q in range(2):
        fourth_copy(q, 1).wait_recv()
        pair_copy(q, 1).start()
        pair_copy(q, 3).start()
    for q in range(2):
        fourth_copy(q, 2).wait_recv()
        pair_copy(q, 2).start()
    for q in range(2):
        for n in range(4):
            pair_copy(q, n).wait_recv()
    for k in range(2):
        at = 0
        for i in range(4):
            for n in range(4 - i):
                j = 2 * (i + n) + k
                block = full[k, at:at + PANEL]
                G[i * PANEL:(i + 1) * PANEL, j * LANES:(j + 1) * LANES] = block
                if n:
                    G[j * LANES:(j + 1) * LANES, i * PANEL:(i + 1) * PANEL] = block.T
                at += PANEL

    def product(lhs, rhs, out, finish):
        for i in range(4):
            low, high = i * PANEL, (i + 1) * PANEL
            v = jnp.dot(lhs[low:high], rhs[:, low:], preferred_element_type=F32)
            v = finish(v, slice(low, high), slice(low, FF)).astype(BF16)
            out[low:high, low:] = v
            for j in range(i + 1, 4):
                out[j * PANEL:(j + 1) * PANEL, low:high] = v[:, (j - i) * PANEL:(j - i + 1) * PANEL].T

    def polynomial(src, q, t, out, scale):
        b_s = COEF_B * scale
        c_s = COEF_C * scale * scale
        product(src, src, q, lambda v, i, j: b_s * src[i, j].astype(F32) + c_s * v)
        product(src, q, t, lambda v, i, j: scale * (COEF_A * src[i, j].astype(F32) + v))
        product(t, q, out, lambda v, i, j: COEF_A * t[i, j].astype(F32) + v)

    def advance(src, rhs, scale):
        v = src[...]
        w = scale * (COEF_A * v.astype(F32) + jnp.dot(v, rhs[...], preferred_element_type=F32))
        return w.astype(BF16)

    for n in range(2):
        X2[0, n * BLOCK:(n + 1) * BLOCK] = X[2 * c + n]
    polynomial(G, A, B, T, inv * inv)
    X2[1] = advance(X2.at[0], A, inv)
    polynomial(T, A, B, G, 1.0)
    X2[0] = advance(X2.at[1], A, 1.0)
    v = X2[0]
    w = jnp.dot(v, G[...], preferred_element_type=F32).astype(BF16)
    z = jnp.dot(w, G[...], preferred_element_type=F32)
    z = (COEF_A * v.astype(F32) + COEF_B * w.astype(F32) + COEF_C * z).astype(BF16)

    def return_copy(n, dc):
        src = back.at[n, lax.rem(c + dc, 2)]
        return remote(src, ret.at[e], bs.at[n, dc], br.at[e], target(2 * c + n, x, y, lax.rem(c + dc, 2)))

    def return_local(n):
        return pltpu.make_async_copy(back.at[n, c], ret.at[e], bl.at[0])

    def return_in(m):
        return remote(back.at[0, 0], ret.at[m], bs.at[0, 0], br.at[m], in_column(0, 1))

    for n in range(2):
        for h in range(2):
            for k in range(2):
                top = n * BLOCK + h * ROWS
                back[n, h, k * ROWS:(k + 1) * ROWS] = z[top:top + ROWS, k * HALF:(k + 1) * HALF]
        return_copy(n, 1).start()

        @pl.when(2 * c + n != e)
        def _():
            return_copy(n, 0).start()

        @pl.when(2 * c + n == e)
        def _():
            return_local(n).start()

    for dz in range(4):
        for dc in range(2):
            if dz + dc:
                slot_copy(dz, dc).wait_recv()
            else:
                slot_copy(0, 0).wait()

    def momentum(i, carry):
        for h in range(2):
            cols = pl.ds(h * HALF, HALF)
            buf[i, :, cols] = MOMENT * buf[i, :, cols] + factor * zin2[i, h].astype(F32)
        return carry

    lax.fori_loop(0, GROUPS, momentum, 0)
    new_own = pltpu.make_async_copy(buf.at[:, mine_rows], new_mom.at[c], ns.at[0])
    new_sib = remote(buf.at[:, other_rows], new_mom.at[c], ns.at[1], ns.at[2], in_column(0, 1))
    new_sib.start()
    new_own.start()

    for copy in spread:
        copy.wait_recv()
    lane = lax.broadcasted_iota(jnp.int32, (8, LANES), 1)
    mean_sq = jnp.zeros((8, LANES), F32)
    for m in range(MATS):
        mean_sq = mean_sq + jnp.where(lane == m, whole_sum(sq_in[2 * m]) / float(D * FF), 0.0)
    rms_out[...] = jnp.sqrt(mean_sq)

    def drain(k, carry):
        for m in range(MATS):
            sib_copy(k, m).wait_send()
            for which in range(3):
                copy1(k, m, which).wait_send()

                @pl.when(k < LAST)
                def _():
                    copy2(k, m, which).wait_send()

                @pl.when(k == LAST)
                def _():
                    copy2_last(m, which).wait_send()
        for dz, dc in COLUMN:
            z_copy(k, dz, dc).wait_send()
        return carry

    lax.fori_loop(0, CHUNKS, drain, 0)
    for dz in (1, 2, 3):
        mom_copy(dz).wait_send()
    mom_pass.wait_send()
    mom_sib.wait_send()
    for q in range(2):
        for n in range(3):
            first_copy(q, n).wait_send()
            second_copy(q, n + 1).wait_send()
            third_copy(q, n + 1).wait_send()
            fourth_copy(q, n).wait_send()
        for n in range(4):
            pair_copy(q, n).wait_send()
    for dz, dc in COLUMN:
        slot_copy(dz, dc).wait_send()
    for copy in first + second + squares + spread:
        copy.wait_send()
    for dz in (0, 1, 3, 2):
        m = wrap(e + dz)
        if dz:
            return_in(m).wait_recv()
        else:
            @pl.when(e // 2 == c)
            def _():
                return_local(0).wait()

            @pl.when(e // 2 != c)
            def _():
                return_in(m).wait_recv()
        v = ret[m].astype(F32)
        rows_out[m, :, :HALF] = v[:ROWS].astype(BF16)
        rows_out[m, :, HALF:] = v[ROWS:].astype(BF16)
    for n in range(2):
        return_copy(n, 1).wait_send()

        @pl.when(2 * c + n != e)
        def _():
            return_copy(n, 0).wait_send()

    new_own.wait()
    new_sib.wait()


ANY = pl.BlockSpec(memory_space=pl.ANY)
VMEM = pl.BlockSpec(memory_space=pltpu.VMEM)
SMEM = pl.BlockSpec(memory_space=pltpu.SMEM)
DMA = pltpu.SemaphoreType.DMA


def per_device(grad_terms, momentum, weights, owner_list):
    small = (CHUNKS, MATS, STRIP, HALF)
    large = (CHUNKS, MATS, SIDE, STRIP, HALF)
    whole = (MATS, SIDE, SIDE, BLOCK, HALF)
    tile = pltpu.VMEM((8, LANES), F32)
    square = pltpu.VMEM((FF, FF), BF16)
    new_mom, rows, rms = pl.pallas_call(
        muon_kernel,
        name="muon",
        out_shape=(
            jax.ShapeDtypeStruct((SLOTS, GROUPS, ROWS, FF), F32),
            jax.ShapeDtypeStruct((MATS, ROWS, FF), BF16),
            jax.ShapeDtypeStruct((8, LANES), F32),
        ),
        in_specs=[SMEM, ANY, ANY],
        out_specs=(ANY, VMEM, VMEM),
        scratch_shapes=[
            pltpu.VMEM(whole, BF16), pltpu.VMEM(whole, BF16),
            pltpu.VMEM(large, BF16), pltpu.VMEM(large, BF16), pltpu.VMEM(large, BF16), pltpu.VMEM(large, BF16),
            pltpu.VMEM(small, BF16), pltpu.VMEM(small, BF16), pltpu.VMEM(small, BF16),
            pltpu.VMEM((MATS, BLOCK, HALF), BF16),
            pltpu.VMEM((GROUPS, 2, BLOCK, HALF), BF16),
            pltpu.VMEM((GROUPS * SLOTS, BLOCK, HALF), BF16),
            pltpu.VMEM((GROUPS, 2, BLOCK, HALF), BF16),
            pltpu.VMEM((SLOTS, GROUPS, ROWS, FF), F32),
            pltpu.VMEM((4, GROUPS, BLOCK, HALF), BF16), pltpu.VMEM((4, GROUPS, BLOCK, HALF), BF16),
            pltpu.VMEM((2, GROUPS, BLOCK, HALF), BF16),
            pltpu.VMEM((GROUPS, BLOCK, FF), F32),
            pltpu.VMEM((GROUPS, BLOCK, FF), BF16),
            pltpu.VMEM((GROUPS * BLOCK, HALF), BF16),
            pltpu.VMEM((2, 2 * BLOCK, FF), BF16),
            pltpu.VMEM((32 * PART, LANES), BF16), pltpu.VMEM((2, 32 * PART, LANES), BF16),
            pltpu.VMEM((2, 3, 4 * PART, LANES), BF16),
            pltpu.VMEM((2, 4 * PART, LANES), BF16),
            pltpu.VMEM((2, 4 * PART, LANES), BF16),
            pltpu.VMEM((2, 3, PART, LANES), BF16),
            pltpu.VMEM((2, PART, LANES), BF16),
            square, square, square, square,
            pltpu.VMEM((2, 2, BLOCK, HALF), BF16), pltpu.VMEM((MATS, BLOCK, HALF), BF16),
            tile, tile, tile, tile,
            pltpu.VMEM((8, 8, LANES), F32), pltpu.VMEM((16, 8, LANES), F32), pltpu.VMEM((16, 8, LANES), F32),
            pltpu.VMEM((8, 8, LANES), F32),
            DMA((CHUNKS, MATS)), DMA((CHUNKS, MATS)), DMA((CHUNKS, MATS)),
            DMA((CHUNKS, MATS, 3)), DMA((CHUNKS, MATS, 3)), DMA((CHUNKS, MATS, 3)), DMA((CHUNKS, MATS, 3)),
            DMA((CHUNKS, 8)), DMA((CHUNKS, 8)), DMA((CHUNKS,)), DMA((4,)), DMA((4,)), DMA((4,)), DMA((2,)),
            DMA((7,)), DMA((7,)), DMA((15,)), DMA((15,)), DMA((3,)),
            DMA((2, 3)), DMA((2, 3)), DMA((2, 3)), DMA((2, 3)), DMA((2, 3)), DMA((2, 3)), DMA((2, 3)), DMA((2, 3)),
            DMA((2, 4)), DMA((2, 4)),
            DMA((15,)), DMA((15,)), DMA((7,)), DMA((7,)), DMA((8,)), DMA((8,)), DMA((2, 2)), DMA((4,)), DMA((1,)),
        ],
        compiler_params=pltpu.CompilerParams(collective_id=0, has_side_effects=True, vmem_limit_bytes=60 << 20),
    )(owner_list, grad_terms.reshape(MATS, SIDE, SIDE, BLOCK, FF), momentum[0])

    rows = rows.astype(F32)
    scale_rms = 0.2 * math.sqrt(max(D, FF))
    update = (scale_rms * rows).astype(BF16)
    new_weights = weights * (1.0 - LEARN * DECAY) - LEARN * scale_rms * rows
    return (new_weights, update, new_mom[None], rms[0, :MATS])


def solution(mesh):
    placed = (
        P("dp", None, "expert", None),
        P("expert", None, None, "dp", None),
        P(None, ("expert", "dp"), None),
        P(),
    )
    return jax.shard_map(
        per_device,
        mesh=mesh,
        in_specs=placed,
        out_specs=(
            P(None, ("expert", "dp"), None),
            P(None, ("expert", "dp"), None),
            P("expert", None, None, "dp", None),
            P(),
        ),
        check_vma=False,
    )
```

time: 123 us -> 117 us (0.951)
  Pallas kernels: 118 us -> 112 us
    pallas_call x1, Pallas kernels: 118 us -> 112 us  [per_device(): pl.pallas_call(muon_kernel, name='muon', out_shape=(jax.ShapeDtypeStruct(...]
where the time goes in v3:
time: 117 us
  Pallas kernels  112 us (96%)
  local copies, waits for them, and re-layouts  2.56 us (2%)
  other arithmetic  2.31 us (2%)
    pallas_call x1, Pallas kernels, per_device(): pl.pallas_call(muon_kernel, name='muon', out_shape=(jax.ShapeDtypeStruct(...  112 us

profile of v3, /device:TPU:1, one launch (start us, length us, event | category | flops | bytes accessed | tf_op | source)
XLA Modules:
  0.0 117.3 jit_solution(14716241107562896321)
XLA Ops:
  0.6 0.0 copy-start.1
  0.6 111.7 %muon.1 = (f32[2,4,56,1024]{3,2,1,0:T(8,128)}, bf16[4,56,1024]{2,1,0:T(8,128)(2,1)}, f32[8,128]{1,0:T(8,128)}) custom-call(s32[4]{0:T(128)} %owners.1, bf16[4,4,4,112,1024]{4,3,2,1,0:T(8,128)(2,1)} %bitcast.5, f32[2,4,56,1024]{3,2,1,0:T(8,128)} %bitcast.6), custom_call_target="tpu_custom_call" | custom-call | tf_op jit(solution)/shard_map/muon/pallas_call | solution.py:622
  112.4 0.0 copy-start
  112.4 1.3 %slice_bitcast_fusion = f32[4]{0:T(128)} fusion(f32[8,128]{1,0:T(8,128)} %get-tuple-element.9), kind=kLoop, calls=%fused_computation.4 | loop fusion | bytes 32 | tf_op jit(solution)/shard_map/squeeze | solution.py:673
  113.7 0.0 copy-done.1
  113.7 2.3 %fusion.1 = (bf16[4,56,1024]{2,1,0:T(8,128)(2,1)}, f32[4,56,1024]{2,1,0:T(8,128)}) fusion(bf16[4,56,1024]{2,1,0:T(8,128)(2,1)} %get-tuple-element.7, f32[4,56,1024]{2,1,0:T(8,128)S(1)} %copy-done.1), kind=kLoop, calls=%fused_computation.3 | loop fusion | flops 1376256 | bytes 2752512 | tf_op jit(solution)/shard_map/convert_element_type | solution.py:671
  116.0 0.0 copy-done
  116.0 1.2 %copy.9 = f32[1,2,4,56,1024]{4,3,2,1,0:T(8,128)} copy(f32[1,2,4,56,1024]{4,3,2,1,0:T(8,128)S(1)} %bitcast.7) | data formatting | bytes 3670016
Async XLA Ops:
  0.6 113.1 %copy-start.1 = (f32[4,56,1024]{2,1,0:T(8,128)S(1)}, f32[4,56,1024]{2,1,0:T(8,128)}, u32[]{:S(2)}) copy-start(f32[4,56,1024]{2,1,0:T(8,128)} %param.6) | copy-start | bytes 2752516
  112.4 3.7 %copy-start = (f32[2,4,56,1024]{3,2,1,0:T(8,128)S(1)}, f32[2,4,56,1024]{3,2,1,0:T(8,128)}, u32[]{:S(2)}) copy-start(f32[2,4,56,1024]{3,2,1,0:T(8,128)} %get-tuple-element.8) | copy-start | bytes 5505028

commit v4 on v3

--- a/solution.py
+++ b/solution.py
@@ -20,6 +20,7 @@
 STRIP = 16
 CHUNKS = BLOCK // STRIP
 LAST = CHUNKS - 1
+SHORT = 5
 PANEL = 256
 PART = 80
 
@@ -57,10 +58,10 @@
 
 def muon_kernel(owners, g, mom, new_mom, rows_out, rms_out,
                 own, sib, tr1, dr1, cb1, mid, tr2, dr2, cb2, grad, zin, zout, zin2, momv, mout, min_, mall, buf, X, Xc, X2,
-                packed, full, rs1, cbg, midg, rs2, out2, G, A, B, T, back, ret, acc, acc2, acc3, acc4,
+                packed, full, rs1, midg, rs2, G, A, B, T, back, ret, acc, acc2, acc3, acc4,
                 column, plane, plane2, sq_in,
                 own_s, sib_s, sib_r, s1, r1, s2, r2, zs, zr, zl, ms, m1s, m1r, m2s, cs, cr, ps, pr, ns, g1s, g1r, g2s,
-                g2r, g3s, g3r, g4s, g4r, g5s, g5r, ps2, pr2, qs, qr, z2s, z2r, bs, br, bl):
+                g2r, g3s, g3r, g5s, g5r, ps2, pr2, qs, qr, z2s, z2r, bs, br, bl):
     e = lax.axis_index("expert")
     p = lax.axis_index("dp")
     x, y, c = p // 8, (p // 2) % 4, p % 2
@@ -116,11 +117,11 @@
         i = wrap(pos + (2, -d, d)[which])
         return remote(mid.at[k, m, i], (tr2, dr2, cb2)[which].at[k, m], s2.at[k, m, which], r2.at[k, m, which], dev)
 
-    def copy2_last(m, which):
+    def copy2_short(k, m, which):
         step = (2, 1, 3)[which]
         pos, dev = along(m, False, step)
-        return remote(mid.at[LAST, m, wrap(pos + step)], (tr2, dr2, cb2)[which].at[LAST, m], s2.at[LAST, m, which],
-                      r2.at[LAST, m, which], dev)
+        return remote(mid.at[k, m, wrap(pos + step)], (tr2, dr2, cb2)[which].at[k, m], s2.at[k, m, which],
+                      r2.at[k, m, which], dev)
 
     def z_copy(k, dz, dc):
         j = 2 * dz + dc
@@ -197,15 +198,15 @@
                 v = (to[j].astype(F32) + more[j].astype(F32)) + (came[j].astype(F32) + came2[j].astype(F32))
                 mid[k, m, j] = v.astype(BF16)
 
-            @pl.when(k < LAST)
+            @pl.when(k < SHORT)
             def _():
                 copy2(k, m, 0).start()
                 copy2(k, m, 1).start()
 
-            @pl.when(k == LAST)
+            @pl.when(k >= SHORT)
             def _():
                 for which in range(3):
-                    copy2_last(m, which).start()
+                    copy2_short(k, m, which).start()
 
     def combine2(k):
         for m in range(MATS):
@@ -234,6 +235,14 @@
             pos, _ = along(m, False, 1)
             collect(k, m, mid[k, m, pos].astype(F32) + (dr2[k, m].astype(F32) + cb2[k, m].astype(F32)))
         send_strips(k)
+
+    def finish_short(k):
+        for m in range(MATS):
+            for which in range(3):
+                copy2_short(k, m, which).wait_recv()
+            pos, _ = along(m, False, 1)
+            v = mid[k, m, pos].astype(F32) + tr2[k, m].astype(F32)
+            collect(k, m, v + (dr2[k, m].astype(F32) + cb2[k, m].astype(F32)))
 
     def mom_send(k):
         mom_load.wait()
@@ -264,23 +273,24 @@
             mall[c, i] = v.astype(BF16)
         mom_pass.start()
 
-    stages = ((transit, 0, CHUNKS), (combine, 1, CHUNKS), (direct, 2, CHUNKS), (turn, 3, CHUNKS),
-              (combine2, 4, LAST), (finish_sum, 5, LAST), (mom_send, 1, 1), (mom_sum, LAST + 2, 1))
+    def finish_send(k):
+        finish_short(k)
+        send_strips(k)
+
+    stages = ((transit, 0, 0, CHUNKS), (combine, 1, 0, CHUNKS), (direct, 2, 0, CHUNKS), (turn, 3, 0, CHUNKS),
+              (combine2, 4, 0, SHORT), (finish_sum, 5, 0, SHORT), (finish_send, 4, SHORT, LAST), (mom_send, 1, 0, 1),
+              (mom_sum, LAST + 2, 0, 1))
 
     def step(t, carry):
-        for stage, lag, chunks in stages:
-            @pl.when((t >= lag) & (t < chunks + lag))
-            def _():
-                stage(t - lag)
+        for stage, lag, low, high in stages:
+            if low < high:
+                @pl.when((t >= low + lag) & (t < high + lag))
+                def _():
+                    stage(t - lag)
         return carry
 
     lax.fori_loop(0, LAST + 5, step, 0)
-    for m in range(MATS):
-        for which in range(3):
-            copy2_last(m, which).wait_recv()
-        pos, _ = along(m, False, 1)
-        v = mid[LAST, m, pos].astype(F32) + tr2[LAST, m].astype(F32)
-        collect(LAST, m, v + (dr2[LAST, m].astype(F32) + cb2[LAST, m].astype(F32)))
+    finish_short(LAST)
 
     me_column = 2 * e + c
     me_plane = 4 * x + y
@@ -335,36 +345,26 @@
 
     lax.fori_loop(0, GROUPS, direction, 0)
 
-    d = 2 * c - 1
 
     def part4(ref, q, i):
         return ref.at[pl.ds(pl.multiple_of((4 * q + i) * 4 * PART, 16), 4 * PART)]
 
-    def part1(ref, q, i, j):
-        return ref.at[pl.ds(pl.multiple_of((16 * q + 4 * i + j) * PART, 16), PART)]
-
     def on(q, first, step):
         return (x, in_plane(step, 0)) if (q == 0) == first else (y, in_plane(0, step))
 
-    def first_copy(q, which):
-        pos, dev = on(q, True, -d if which == 1 else d)
-        src = cbg.at[q] if which == 2 else part4(packed, q, wrap(pos + (2, -d)[which]))
-        return remote(src, rs1.at[q, which], g1s.at[q, which], g1r.at[q, which], dev)
+    def first_copy(q, step):
+        pos, dev = on(q, True, step)
+        return remote(part4(packed, q, wrap(pos + step)), rs1.at[q, step - 1], g1s.at[q, step - 1], g1r.at[q, step - 1],
+                      dev)
 
     def second_copy(q, step):
-        pos, dev = on(q, False, step)
-        src = midg.at[q, pl.ds(pl.multiple_of(wrap(pos + step) * PART, 16), PART)]
-        return remote(src, rs2.at[q, step - 1], g2s.at[q, step - 1], g2r.at[q, step - 1], dev)
+        _, dev = on(q, False, step)
+        return remote(midg.at[q], rs2.at[q, step - 1], g2s.at[q, step - 1], g2r.at[q, step - 1], dev)
 
     def third_copy(q, step):
-        pos1, _ = on(q, True, 1)
-        pos2, dev = on(q, False, step)
-        return remote(out2.at[q], part1(full.at[c], q, pos1, pos2), g3s.at[q, step - 1], g3r.at[q, step - 1], dev)
-
-    def fourth_copy(q, which):
-        pos, dev = on(q, True, -d if which == 1 else d)
-        ref = part4(full.at[c], q, wrap(pos - d) if which == 2 else pos)
-        return remote(ref, ref, g4s.at[q, which], g4r.at[q, which], dev)
+        pos, dev = on(q, True, step)
+        ref = part4(full.at[c], q, pos)
+        return remote(ref, ref, g3s.at[q, step - 1], g3r.at[q, step - 1], dev)
 
     def pair_copy(q, n):
         pos, _ = on(q, True, 1)
@@ -384,17 +384,11 @@
             packed[at:at + PANEL] = panel[:, j * LANES:(j + 1) * LANES]
             at += PANEL
         if i in (1, 3):
-            first_copy(i // 2, 0).start()
-            first_copy(i // 2, 1).start()
+            for s in STEPS:
+                first_copy(i // 2, s).start()
     squares = spread_plane(acc3, plane2, ps2, pr2)
     mom_own.wait()
     mom_sib.wait_recv()
-    for q in range(2):
-        first_copy(q, 0).wait_recv()
-        pos, _ = on(q, True, 1)
-        mine = part4(packed, q, wrap(pos + d))
-        cbg[q] = (mine[...].astype(F32) + rs1[q, 0].astype(F32)).astype(BF16)
-        first_copy(q, 2).start()
 
     def slot_copy(dz, dc):
         j = 2 * dz + dc
@@ -411,44 +405,46 @@
             zout[2 * dz + dc] = v.astype(BF16)
             slot_copy(dz, dc).start()
 
+    def drain(k, carry):
+        for m in range(MATS):
+            sib_copy(k, m).wait_send()
+            for which in range(3):
+                copy1(k, m, which).wait_send()
+
+                copy2(k, m, which).wait_send()
+        for dz, dc in COLUMN:
+            z_copy(k, dz, dc).wait_send()
+        return carry
+
+    lax.fori_loop(0, CHUNKS, drain, 0)
+    for dz in (1, 2, 3):
+        mom_copy(dz).wait_send()
+    mom_pass.wait_send()
+    mom_sib.wait_send()
     for q in range(2):
-        first_copy(q, 1).wait_recv()
-        first_copy(q, 2).wait_recv()
+        for s in STEPS:
+            first_copy(q, s).wait_recv()
         pos, _ = on(q, True, 1)
-        mine = part4(packed, q, pos)
-        midg[q] = (mine[...].astype(F32) + (rs1[q, 1].astype(F32) + rs1[q, 2].astype(F32))).astype(BF16)
+        v = part4(packed, q, pos)[...].astype(F32) + rs1[q, 0].astype(F32)
+        midg[q] = (v + (rs1[q, 1].astype(F32) + rs1[q, 2].astype(F32))).astype(BF16)
         for s in STEPS:
             second_copy(q, s).start()
     for q in range(2):
         for s in STEPS:
             second_copy(q, s).wait_recv()
-        pos1, _ = on(q, True, 1)
-        pos2, _ = on(q, False, 1)
-        v = midg[q, pl.ds(pl.multiple_of(pos2 * PART, 16), PART)].astype(F32) + rs2[q, 0].astype(F32)
-        v = (v + (rs2[q, 1].astype(F32) + rs2[q, 2].astype(F32))).astype(BF16)
-        out2[q] = v
+        pos, _ = on(q, True, 1)
+        v = midg[q].astype(F32) + rs2[q, 0].astype(F32)
+        part4(full.at[c], q, pos)[...] = (v + (rs2[q, 1].astype(F32) + rs2[q, 2].astype(F32))).astype(BF16)
         for s in STEPS:
             third_copy(q, s).start()
-        part1(full.at[c], q, pos1, pos2)[...] = v
+        pair_copy(q, 0).start()
     acc4[...] = total_of(squares, plane2, 16)
     spread = spread_column(acc4, sq_in, qs, qr)
     inv = 1.0 / (jnp.sqrt(whole_sum(acc4[...])) + NORM_EPS)
-    for q in range(2):
-        for s in STEPS:
+    for s in (1, 3, 2):
+        for q in range(2):
             third_copy(q, s).wait_recv()
-        fourth_copy(q, 0).start()
-        fourth_copy(q, 1).start()
-        pair_copy(q, 0).start()
-    for q in range(2):
-        fourth_copy(q, 0).wait_recv()
-        fourth_copy(q, 2).start()
-    for q in range(2):
-        fourth_copy(q, 1).wait_recv()
-        pair_copy(q, 1).start()
-        pair_copy(q, 3).start()
-    for q in range(2):
-        fourth_copy(q, 2).wait_recv()
-        pair_copy(q, 2).start()
+            pair_copy(q, 4 - s).start()
     for q in range(2):
         for n in range(4):
             pair_copy(q, n).wait_recv()
@@ -547,34 +543,11 @@
         mean_sq = mean_sq + jnp.where(lane == m, whole_sum(sq_in[2 * m]) / float(D * FF), 0.0)
     rms_out[...] = jnp.sqrt(mean_sq)
 
-    def drain(k, carry):
-        for m in range(MATS):
-            sib_copy(k, m).wait_send()
-            for which in range(3):
-                copy1(k, m, which).wait_send()
-
-                @pl.when(k < LAST)
-                def _():
-                    copy2(k, m, which).wait_send()
-
-                @pl.when(k == LAST)
-                def _():
-                    copy2_last(m, which).wait_send()
-        for dz, dc in COLUMN:
-            z_copy(k, dz, dc).wait_send()
-        return carry
-
-    lax.fori_loop(0, CHUNKS, drain, 0)
-    for dz in (1, 2, 3):
-        mom_copy(dz).wait_send()
-    mom_pass.wait_send()
-    mom_sib.wait_send()
     for q in range(2):
-        for n in range(3):
-            first_copy(q, n).wait_send()
-            second_copy(q, n + 1).wait_send()
-            third_copy(q, n + 1).wait_send()
-            fourth_copy(q, n).wait_send()
+        for s in STEPS:
+            first_copy(q, s).wait_send()
+            second_copy(q, s).wait_send()
+            third_copy(q, s).wait_send()
         for n in range(4):
             pair_copy(q, n).wait_send()
     for dz, dc in COLUMN:
@@ -647,9 +620,7 @@
             pltpu.VMEM((32 * PART, LANES), BF16), pltpu.VMEM((2, 32 * PART, LANES), BF16),
             pltpu.VMEM((2, 3, 4 * PART, LANES), BF16),
             pltpu.VMEM((2, 4 * PART, LANES), BF16),
-            pltpu.VMEM((2, 4 * PART, LANES), BF16),
-            pltpu.VMEM((2, 3, PART, LANES), BF16),
-            pltpu.VMEM((2, PART, LANES), BF16),
+            pltpu.VMEM((2, 3, 4 * PART, LANES), BF16),
             square, square, square, square,
             pltpu.VMEM((2, 2, BLOCK, HALF), BF16), pltpu.VMEM((MATS, BLOCK, HALF), BF16),
             tile, tile, tile, tile,
@@ -659,7 +630,7 @@
             DMA((CHUNKS, MATS, 3)), DMA((CHUNKS, MATS, 3)), DMA((CHUNKS, MATS, 3)), DMA((CHUNKS, MATS, 3)),
             DMA((CHUNKS, 8)), DMA((CHUNKS, 8)), DMA((CHUNKS,)), DMA((4,)), DMA((4,)), DMA((4,)), DMA((2,)),
             DMA((7,)), DMA((7,)), DMA((15,)), DMA((15,)), DMA((3,)),
-            DMA((2, 3)), DMA((2, 3)), DMA((2, 3)), DMA((2, 3)), DMA((2, 3)), DMA((2, 3)), DMA((2, 3)), DMA((2, 3)),
+            DMA((2, 3)), DMA((2, 3)), DMA((2, 3)), DMA((2, 3)), DMA((2, 3)), DMA((2, 3)),
             DMA((2, 4)), DMA((2, 4)),
             DMA((15,)), DMA((15,)), DMA((7,)), DMA((7,)), DMA((8,)), DMA((8,)), DMA((2, 2)), DMA((4,)), DMA((1,)),
         ],

time: 117 us -> 112 us (0.957)
  Pallas kernels: 112 us -> 106 us
    pallas_call x1, Pallas kernels: 112 us -> 106 us  [per_device(): pl.pallas_call(muon_kernel, name='muon', out_shape=(jax.ShapeDtypeStruct(...]
where the time goes in v4:
time: 112 us; the launch traced here: 111 us
  Pallas kernels  106 us (95%)
  local copies, waits for them, and re-layouts  2.56 us (2%)
  other arithmetic  2.31 us (2%)
    pallas_call x1, Pallas kernels, per_device(): pl.pallas_call(muon_kernel, name='muon', out_shape=(jax.ShapeDtypeStruct(...  106 us
    convert_element_type x1, other arithmetic, per_device(): update = (scale_rms * rows).astype(BF16)  2.31 us

profile of v4, /device:TPU:1, one launch (start us, length us, event | category | flops | bytes accessed | tf_op | source)
XLA Modules:
  0.0 111.4 jit_solution(16526884959631234345)
XLA Ops:
  0.6 0.0 copy-start.1
  0.6 105.9 %muon.1 = (f32[2,4,56,1024]{3,2,1,0:T(8,128)}, bf16[4,56,1024]{2,1,0:T(8,128)(2,1)}, f32[8,128]{1,0:T(8,128)}) custom-call(s32[4]{0:T(128)} %owners.1, bf16[4,4,4,112,1024]{4,3,2,1,0:T(8,128)(2,1)} %bitcast.5, f32[2,4,56,1024]{3,2,1,0:T(8,128)} %bitcast.6), custom_call_target="tpu_custom_call" | custom-call | tf_op jit(solution)/shard_map/muon/pallas_call | solution.py:595
  106.6 0.0 copy-start
  106.6 1.3 %slice_bitcast_fusion = f32[4]{0:T(128)} fusion(f32[8,128]{1,0:T(8,128)} %get-tuple-element.9), kind=kLoop, calls=%fused_computation.4 | loop fusion | bytes 32 | tf_op jit(solution)/shard_map/squeeze | solution.py:644
  107.9 0.0 copy-done.1
  107.9 2.3 %fusion.1 = (bf16[4,56,1024]{2,1,0:T(8,128)(2,1)}, f32[4,56,1024]{2,1,0:T(8,128)}) fusion(bf16[4,56,1024]{2,1,0:T(8,128)(2,1)} %get-tuple-element.7, f32[4,56,1024]{2,1,0:T(8,128)S(1)} %copy-done.1), kind=kLoop, calls=%fused_computation.3 | loop fusion | flops 1376256 | bytes 2752512 | tf_op jit(solution)/shard_map/convert_element_type | solution.py:642
  110.2 0.0 copy-done
  110.2 1.2 %copy.9 = f32[1,2,4,56,1024]{4,3,2,1,0:T(8,128)} copy(f32[1,2,4,56,1024]{4,3,2,1,0:T(8,128)S(1)} %bitcast.7) | data formatting | bytes 3670016
Async XLA Ops:
  0.6 107.3 %copy-start.1 = (f32[4,56,1024]{2,1,0:T(8,128)S(1)}, f32[4,56,1024]{2,1,0:T(8,128)}, u32[]{:S(2)}) copy-start(f32[4,56,1024]{2,1,0:T(8,128)} %param.6) | copy-start | bytes 2752516
  106.6 3.7 %copy-start = (f32[2,4,56,1024]{3,2,1,0:T(8,128)S(1)}, f32[2,4,56,1024]{3,2,1,0:T(8,128)}, u32[]{:S(2)}) copy-start(f32[2,4,56,1024]{3,2,1,0:T(8,128)} %get-tuple-element.8) | copy-start | bytes 5505028

commit v5 on v4

--- a/solution.py
+++ b/solution.py
@@ -57,11 +57,11 @@
 
 
 def muon_kernel(owners, g, mom, new_mom, rows_out, rms_out,
-                own, sib, tr1, dr1, cb1, mid, tr2, dr2, cb2, grad, zin, zout, zin2, momv, mout, min_, mall, buf, X, Xc, X2,
+                own, sib, tr1, dc1, mid, tr2, dc2, grad, zin, zout, zin2, momv, mout, min_, mall, Mb, gright, mright, grams, buf, X, X2,
                 packed, full, rs1, midg, rs2, G, A, B, T, back, ret, acc, acc2, acc3, acc4,
                 column, plane, plane2, sq_in,
-                own_s, sib_s, sib_r, s1, r1, s2, r2, zs, zr, zl, ms, m1s, m1r, m2s, cs, cr, ps, pr, ns, g1s, g1r, g2s,
-                g2r, g3s, g3r, g5s, g5r, ps2, pr2, qs, qr, z2s, z2r, bs, br, bl):
+                own_s, sib_s, sib_r, s1, t1r, d1r, s2, t2r, d2r, zs, zr, zl, ms, m1s, m1r, m2s, cs, cr, ps, pr, ns, g1s, g1r,
+                g2s, g2r, g3s, g3r, g5s, g5r, ps2, pr2, qs, qr, z2s, z2r, z2l, bs, br, bl):
     e = lax.axis_index("expert")
     p = lax.axis_index("dp")
     x, y, c = p // 8, (p // 2) % 4, p % 2
@@ -75,6 +75,12 @@
 
     def in_plane(dx, dy):
         return target(e, wrap(x + dx), wrap(y + dy), c)
+
+    def arrived(sem, ref):
+        remote(ref, ref, sem, sem, in_column(0, 1)).wait_recv()
+
+    def left(sem, ref):
+        remote(ref, ref, sem, sem, in_column(0, 1)).wait_send()
 
     places = []
     for m in range(MATS):
@@ -89,13 +95,13 @@
     def strip(k):
         return pl.ds(pl.multiple_of(k * STRIP, STRIP), STRIP)
 
-    def own_copy(k, m):
+    def own_copy(k):
         cols = pl.ds(pl.multiple_of(c * HALF, HALF), HALF)
-        return pltpu.make_async_copy(g.at[m, :, :, strip(k), cols], own.at[m, :, :, strip(k)], own_s.at[k, m])
+        return pltpu.make_async_copy(g.at[:, :, :, strip(k), cols], own.at[:, :, :, strip(k)], own_s.at[k])
 
     def sib_copy(k, m):
         cols = pl.ds(pl.multiple_of(other * HALF, HALF), HALF)
-        return remote(g.at[m, :, :, strip(k), cols], sib.at[m, :, :, strip(k)], sib_s.at[k, m], sib_r.at[k, m],
+        return remote(g.at[m, :, :, strip(k), cols], sib.at[m, :, :, strip(k)], sib_s.at[0], sib_r.at[k, m],
                       in_column(0, 1))
 
     def along(m, first, step):
@@ -109,26 +115,34 @@
         d = sign(m)
         pos, dev = along(m, True, -d if which == 1 else d)
         i = wrap(pos + (2, -d, d)[which])
-        return remote(group(own, k, m, i), (tr1, dr1, cb1)[which].at[k, m], s1.at[k, m, which], r1.at[k, m, which], dev)
+        if which == 0:
+            dst, recv = tr1.at[k, m], t1r.at[k]
+        else:
+            dst, recv = dc1.at[k, m, which - 1], d1r.at[k]
+        return remote(group(own, k, m, i), dst, s1.at[which], recv, dev)
+
+    def ends2(k, m, which):
+        if which == 0:
+            return tr2.at[k, m], s2.at[0], t2r.at[k]
+        return dc2.at[k, m, which - 1], s2.at[which], d2r.at[k]
 
     def copy2(k, m, which):
         d = sign(m)
         pos, dev = along(m, False, -d if which == 1 else d)
         i = wrap(pos + (2, -d, d)[which])
-        return remote(mid.at[k, m, i], (tr2, dr2, cb2)[which].at[k, m], s2.at[k, m, which], r2.at[k, m, which], dev)
+        return remote(mid.at[k, m, i], *ends2(k, m, which), dev)
 
     def copy2_short(k, m, which):
         step = (2, 1, 3)[which]
         pos, dev = along(m, False, step)
-        return remote(mid.at[k, m, wrap(pos + step)], (tr2, dr2, cb2)[which].at[k, m], s2.at[k, m, which],
-                      r2.at[k, m, which], dev)
+        return remote(mid.at[k, m, wrap(pos + step)], *ends2(k, m, which), dev)
 
     def z_copy(k, dz, dc):
         j = 2 * dz + dc
-        src, dst = grad.at[wrap(e + dz), strip(k)], zin.at[e, c, strip(k)]
+        src, dst = grad.at[wrap(e + dz), strip(k)], zin.at[2 * e + c, strip(k)]
         if j == 0:
-            return pltpu.make_async_copy(src, dst, zl.at[k])
-        return remote(src, dst, zs.at[k, j], zr.at[k, j], in_column(dz, dc))
+            return pltpu.make_async_copy(src, dst, zl.at[0])
+        return remote(src, dst, zs.at[0], zr.at[0], in_column(dz, dc))
 
     mine_rows = pl.ds(pl.multiple_of(ROWS * c, 8), ROWS)
     other_rows = pl.ds(pl.multiple_of(ROWS * other, 8), ROWS)
@@ -137,13 +151,12 @@
     mom_sib = remote(mom.at[other], buf.at[:, mine_rows], ms.at[2], ms.at[3], in_column(0, 1))
 
     def mom_copy(dz):
-        return remote(mout.at[dz], min_.at[e], m1s.at[dz], m1r.at[dz], in_column(dz, 0))
+        return remote(mout.at[dz], min_.at[e], m1s.at[0], m1r.at[0], in_column(dz, 0))
 
     mom_pass = remote(mall.at[c], mall.at[c], m2s.at[0], m2s.at[1], in_column(0, 1))
 
     for k in range(CHUNKS):
-        for m in range(MATS):
-            own_copy(k, m).start()
+        own_copy(k).start()
         if k == 0:
             mom_load.start()
     mom_own.start()
@@ -165,16 +178,16 @@
             to[j] = (to[j].astype(F32) + more[j].astype(F32)).astype(BF16)
 
     def transit(k):
-        for m in range(MATS):
-            own_copy(k, m).wait()
+        own_copy(k).wait()
+        for m in range(MATS):
             sib_copy(k, m).wait_recv()
             pos, _ = along(m, True, 1)
             pair_sum(k, m, wrap(pos + 2))
             copy1(k, m, 0).start()
 
     def combine(k):
-        for m in range(MATS):
-            copy1(k, m, 0).wait_recv()
+        arrived(t1r.at[k], tr1.at[k])
+        for m in range(MATS):
             pos, _ = along(m, True, 1)
             i = wrap(pos + sign(m))
             to, more, came = group(own, k, m, i), group(sib, k, m, i), tr1.at[k, m]
@@ -189,11 +202,10 @@
             copy1(k, m, 1).start()
 
     def turn(k):
-        for m in range(MATS):
-            copy1(k, m, 1).wait_recv()
-            copy1(k, m, 2).wait_recv()
+        arrived(d1r.at[k], dc1.at[k])
+        for m in range(MATS):
             pos, _ = along(m, True, 1)
-            to, more, came, came2 = group(own, k, m, pos), group(sib, k, m, pos), dr1.at[k, m], cb1.at[k, m]
+            to, more, came, came2 = group(own, k, m, pos), group(sib, k, m, pos), dc1.at[k, m, 0], dc1.at[k, m, 1]
             for j in range(SIDE):
                 v = (to[j].astype(F32) + more[j].astype(F32)) + (came[j].astype(F32) + came2[j].astype(F32))
                 mid[k, m, j] = v.astype(BF16)
@@ -209,8 +221,8 @@
                     copy2_short(k, m, which).start()
 
     def combine2(k):
-        for m in range(MATS):
-            copy2(k, m, 0).wait_recv()
+        arrived(t2r.at[k], tr2.at[k])
+        for m in range(MATS):
             pos, _ = along(m, False, 1)
             i = wrap(pos + sign(m))
             mid[k, m, i] = (mid[k, m, i].astype(F32) + tr2[k, m].astype(F32)).astype(BF16)
@@ -229,20 +241,19 @@
                 z_copy(k, dz, dc).start()
 
     def finish_sum(k):
-        for m in range(MATS):
-            copy2(k, m, 1).wait_recv()
-            copy2(k, m, 2).wait_recv()
+        arrived(d2r.at[k], dc2.at[k])
+        for m in range(MATS):
             pos, _ = along(m, False, 1)
-            collect(k, m, mid[k, m, pos].astype(F32) + (dr2[k, m].astype(F32) + cb2[k, m].astype(F32)))
+            collect(k, m, mid[k, m, pos].astype(F32) + (dc2[k, m, 0].astype(F32) + dc2[k, m, 1].astype(F32)))
         send_strips(k)
 
     def finish_short(k):
-        for m in range(MATS):
-            for which in range(3):
-                copy2_short(k, m, which).wait_recv()
+        arrived(t2r.at[k], tr2.at[k])
+        arrived(d2r.at[k], dc2.at[k])
+        for m in range(MATS):
             pos, _ = along(m, False, 1)
             v = mid[k, m, pos].astype(F32) + tr2[k, m].astype(F32)
-            collect(k, m, v + (dr2[k, m].astype(F32) + cb2[k, m].astype(F32)))
+            collect(k, m, v + (dc2[k, m, 0].astype(F32) + dc2[k, m, 1].astype(F32)))
 
     def mom_send(k):
         mom_load.wait()
@@ -264,8 +275,7 @@
         mom_sib.start()
 
     def mom_sum(k):
-        for dz in (1, 2, 3):
-            mom_copy(dz).wait_recv()
+        arrived(m1r.at[0], min_.at[pl.ds(0, 3)])
         for i in range(GROUPS):
             v = mout[0, i].astype(F32)
             for dz in (1, 2, 3):
@@ -296,48 +306,106 @@
     me_plane = 4 * x + y
 
     def spread_column(src, dst, send, recv):
-        copies = [remote(src, dst.at[me_column], send.at[i], recv.at[i], in_column(*d)) for i, d in enumerate(COLUMN)]
+        copies = [remote(src, dst.at[me_column], send.at[0], recv.at[0], in_column(*d)) for d in COLUMN]
         for copy in copies:
             copy.start()
         dst[me_column] = src[...]
-        return copies
 
     def spread_plane(src, dst, send, recv):
-        copies = [remote(src, dst.at[me_plane], send.at[i], recv.at[i], in_plane(*d)) for i, d in enumerate(PLANE)]
+        copies = [remote(src, dst.at[me_plane], send.at[0], recv.at[0], in_plane(*d)) for d in PLANE]
         for copy in copies:
             copy.start()
         dst[me_plane] = src[...]
-        return copies
-
-    def total_of(copies, ref, count):
-        for copy in copies:
-            copy.wait_recv()
+
+    def total_of(recv, ref, count):
+        arrived(recv.at[0], ref.at[pl.ds(0, count - 1)])
         v = ref[0]
         for j in range(1, count):
             v = v + ref[j]
         return v
 
-    first = spread_column(acc, column, cs, cr)
+    spread_column(acc, column, cs, cr)
     send_strips(LAST)
-    acc2[...] = total_of(first, column, 8)
-    second = spread_plane(acc2, plane, ps, pr)
+    acc2[...] = total_of(cr, column, 8)
+    spread_plane(acc2, plane, ps, pr)
     mom_pass.wait_recv()
-    for k in range(CHUNKS):
-        for dz in range(4):
-            for dc in range(2):
-                if dz + dc:
-                    z_copy(k, dz, dc).wait_recv()
-                else:
-                    z_copy(k, 0, 0).wait()
-    mean = whole_sum(total_of(second, plane, 16)) / float(MATS * D * FF)
-    factor = jnp.minimum(1.0, CLIP_RMS / jnp.sqrt(mean + MEAN_EPS))
-
-    def direction(i, carry):
+    arrived(zr.at[0], zin.at[pl.ds(0, 7)])
+    pltpu.make_async_copy(zin.at[0], zin.at[0], zl.at[0]).wait()
+
+    def unpack(i, carry):
         parts = [mall[k, i].astype(F32) for k in range(2)]
         for h in range(2):
-            kept = jnp.concatenate([v[h * ROWS:(h + 1) * ROWS] for v in parts], axis=0)
-            v = factor * zin[i, h].astype(F32)
-            v = v + MOMENT * (MOMENT * kept + v)
+            kept_rows = [v[h * ROWS:(h + 1) * ROWS] for v in parts]
+            Mb[i, h] = jnp.concatenate(kept_rows, axis=0).astype(BF16)
+        return carry
+
+    lax.fori_loop(0, GROUPS, unpack, 0)
+    for j in range(4):
+        cols = pl.ds(pl.multiple_of((2 * (j % 2) + c) * LANES, LANES), LANES)
+        gright[:, j * LANES:(j + 1) * LANES] = jnp.concatenate([zin[2 * n + j // 2, :, cols] for n in range(GROUPS)], axis=0)
+        mright[:, j * LANES:(j + 1) * LANES] = Mb[:, j // 2, :, cols].reshape(GROUPS * BLOCK, LANES)
+
+    def outer(left, right):
+        return lax.dot_general(left, right, (((0,), (0,)), ((), ())), preferred_element_type=F32)
+
+    at = 0
+    for i in range(4):
+        cols = slice((i % 2) * PANEL, (i % 2 + 1) * PANEL)
+        gleft = jnp.concatenate([zin[2 * n + i // 2, :, cols] for n in range(GROUPS)], axis=0)
+        mleft = Mb[:, i // 2, :, cols].reshape(GROUPS * BLOCK, PANEL)
+        gr, mr = gright[:, i * LANES:], mright[:, i * LANES:]
+        gg, gm, mm = outer(gleft, gr), outer(gleft, mr) + outer(mleft, gr), outer(mleft, mr)
+        for j in range(4 - i):
+            for n, v in enumerate((gg, gm, mm)):
+                grams[n, at:at + PANEL] = v[:, j * LANES:(j + 1) * LANES]
+            at += PANEL
+    mean = whole_sum(total_of(pr, plane, 16)) / float(MATS * D * FF)
+    factor = jnp.minimum(1.0, CLIP_RMS / jnp.sqrt(mean + MEAN_EPS))
+
+
+    def part4(ref, q, i):
+        return ref.at[pl.ds(pl.multiple_of((4 * q + i) * 4 * PART, 16), 4 * PART)]
+
+    def on(q, first, step):
+        return (x, in_plane(step, 0)) if (q == 0) == first else (y, in_plane(0, step))
+
+    def first_copy(q, step):
+        pos, dev = on(q, True, step)
+        return remote(part4(packed, q, wrap(pos + step)), rs1.at[q, step - 1], g1s.at[0], g1r.at[q],
+                      dev)
+
+    def second_copy(q, step):
+        _, dev = on(q, False, step)
+        return remote(midg.at[q], rs2.at[q, step - 1], g2s.at[0], g2r.at[q], dev)
+
+    def third_copy(q, step):
+        pos, dev = on(q, True, step)
+        ref = part4(full.at[c], q, pos)
+        return remote(ref, ref, g3s.at[0], g3r.at[q, step - 1], dev)
+
+    def pair_copy(q, n):
+        pos, _ = on(q, True, 1)
+        ref = part4(full.at[c], q, wrap(pos + n))
+        return remote(ref, ref, g5s.at[0], g5r.at[0], in_column(0, 1))
+
+    STEPS = (2, 1, 3)
+    u = (1.0 + MOMENT) * factor
+    w = MOMENT * MOMENT
+    for q in range(2):
+        def weigh(i, carry):
+            rows = pl.ds(pl.multiple_of((16 * q + i) * PART, 16), PART)
+            v = (u * u) * grams[0, rows] + (u * w) * grams[1, rows] + (w * w) * grams[2, rows]
+            packed[rows] = v.astype(BF16)
+            return carry
+
+        lax.fori_loop(0, 16, weigh, 0)
+        for s in STEPS:
+            first_copy(q, s).start()
+
+    def direction(i, carry):
+        for h in range(2):
+            v = factor * zin[2 * i + h].astype(F32)
+            v = v + MOMENT * (MOMENT * Mb[i, h].astype(F32) + v)
             X[i, :, h * HALF:(h + 1) * HALF] = v.astype(BF16)
             sq = jnp.sum(jnp.square(v).reshape(BLOCK // 8, 8, HALF), axis=0)
             acc3[...] += sq[:, :128] + sq[:, 128:256] + sq[:, 256:384] + sq[:, 384:]
@@ -345,56 +413,15 @@
 
     lax.fori_loop(0, GROUPS, direction, 0)
 
-
-    def part4(ref, q, i):
-        return ref.at[pl.ds(pl.multiple_of((4 * q + i) * 4 * PART, 16), 4 * PART)]
-
-    def on(q, first, step):
-        return (x, in_plane(step, 0)) if (q == 0) == first else (y, in_plane(0, step))
-
-    def first_copy(q, step):
-        pos, dev = on(q, True, step)
-        return remote(part4(packed, q, wrap(pos + step)), rs1.at[q, step - 1], g1s.at[q, step - 1], g1r.at[q, step - 1],
-                      dev)
-
-    def second_copy(q, step):
-        _, dev = on(q, False, step)
-        return remote(midg.at[q], rs2.at[q, step - 1], g2s.at[q, step - 1], g2r.at[q, step - 1], dev)
-
-    def third_copy(q, step):
-        pos, dev = on(q, True, step)
-        ref = part4(full.at[c], q, pos)
-        return remote(ref, ref, g3s.at[q, step - 1], g3r.at[q, step - 1], dev)
-
-    def pair_copy(q, n):
-        pos, _ = on(q, True, 1)
-        ref = part4(full.at[c], q, wrap(pos + n))
-        return remote(ref, ref, g5s.at[q, n], g5r.at[q, n], in_column(0, 1))
-
-    STEPS = (2, 1, 3)
-    for j in range(4):
-        cols = pl.ds(pl.multiple_of((2 * j + c) * LANES, LANES), LANES)
-        Xc[:, j * LANES:(j + 1) * LANES] = X[:, :, cols].reshape(GROUPS * BLOCK, LANES)
-    at = 0
-    for i in range(4):
-        left = X[:, :, i * PANEL:(i + 1) * PANEL].reshape(GROUPS * BLOCK, PANEL)
-        panel = lax.dot_general(left, Xc[:, i * LANES:], (((0,), (0,)), ((), ())),
-                                preferred_element_type=F32).astype(BF16)
-        for j in range(4 - i):
-            packed[at:at + PANEL] = panel[:, j * LANES:(j + 1) * LANES]
-            at += PANEL
-        if i in (1, 3):
-            for s in STEPS:
-                first_copy(i // 2, s).start()
-    squares = spread_plane(acc3, plane2, ps2, pr2)
+    spread_plane(acc3, plane2, ps2, pr2)
     mom_own.wait()
     mom_sib.wait_recv()
 
     def slot_copy(dz, dc):
         j = 2 * dz + dc
         if j == 0:
-            return pltpu.make_async_copy(zout.at[0], zin2.at[e, c], z2s.at[0])
-        return remote(zout.at[j], zin2.at[e, c], z2s.at[j], z2r.at[j], in_column(dz, dc))
+            return pltpu.make_async_copy(zout.at[0], zin2.at[2 * e + c], z2l.at[0])
+        return remote(zout.at[j], zin2.at[2 * e + c], z2s.at[0], z2r.at[0], in_column(dz, dc))
 
     for dz in (2, 1, 3, 0):
         for dc in range(2):
@@ -405,49 +432,35 @@
             zout[2 * dz + dc] = v.astype(BF16)
             slot_copy(dz, dc).start()
 
-    def drain(k, carry):
-        for m in range(MATS):
-            sib_copy(k, m).wait_send()
-            for which in range(3):
-                copy1(k, m, which).wait_send()
-
-                copy2(k, m, which).wait_send()
-        for dz, dc in COLUMN:
-            z_copy(k, dz, dc).wait_send()
-        return carry
-
-    lax.fori_loop(0, CHUNKS, drain, 0)
-    for dz in (1, 2, 3):
-        mom_copy(dz).wait_send()
-    mom_pass.wait_send()
-    mom_sib.wait_send()
+    left(sib_s.at[0], sib)
+    for which in range(3):
+        left(s1.at[which], tr1)
+        left(s2.at[which], tr2)
+    left(zs.at[0], zin.at[pl.ds(0, 7)])
+    left(m1s.at[0], mout.at[pl.ds(0, 3)])
     for q in range(2):
-        for s in STEPS:
-            first_copy(q, s).wait_recv()
+        arrived(g1r.at[q], rs1.at[q])
         pos, _ = on(q, True, 1)
         v = part4(packed, q, pos)[...].astype(F32) + rs1[q, 0].astype(F32)
         midg[q] = (v + (rs1[q, 1].astype(F32) + rs1[q, 2].astype(F32))).astype(BF16)
         for s in STEPS:
             second_copy(q, s).start()
     for q in range(2):
-        for s in STEPS:
-            second_copy(q, s).wait_recv()
+        arrived(g2r.at[q], rs2.at[q])
         pos, _ = on(q, True, 1)
         v = midg[q].astype(F32) + rs2[q, 0].astype(F32)
         part4(full.at[c], q, pos)[...] = (v + (rs2[q, 1].astype(F32) + rs2[q, 2].astype(F32))).astype(BF16)
         for s in STEPS:
             third_copy(q, s).start()
         pair_copy(q, 0).start()
-    acc4[...] = total_of(squares, plane2, 16)
-    spread = spread_column(acc4, sq_in, qs, qr)
+    acc4[...] = total_of(pr2, plane2, 16)
+    spread_column(acc4, sq_in, qs, qr)
     inv = 1.0 / (jnp.sqrt(whole_sum(acc4[...])) + NORM_EPS)
     for s in (1, 3, 2):
         for q in range(2):
             third_copy(q, s).wait_recv()
             pair_copy(q, 4 - s).start()
-    for q in range(2):
-        for n in range(4):
-            pair_copy(q, n).wait_recv()
+    arrived(g5r.at[0], full.at[other])
     for k in range(2):
         at = 0
         for i in range(4):
@@ -516,17 +529,13 @@
         def _():
             return_local(n).start()
 
-    for dz in range(4):
-        for dc in range(2):
-            if dz + dc:
-                slot_copy(dz, dc).wait_recv()
-            else:
-                slot_copy(0, 0).wait()
+    arrived(z2r.at[0], zin2.at[pl.ds(0, 7)])
+    slot_copy(0, 0).wait()
 
     def momentum(i, carry):
         for h in range(2):
             cols = pl.ds(h * HALF, HALF)
-            buf[i, :, cols] = MOMENT * buf[i, :, cols] + factor * zin2[i, h].astype(F32)
+            buf[i, :, cols] = MOMENT * buf[i, :, cols] + factor * zin2[2 * i + h].astype(F32)
         return carry
 
     lax.fori_loop(0, GROUPS, momentum, 0)
@@ -535,25 +544,24 @@
     new_sib.start()
     new_own.start()
 
-    for copy in spread:
-        copy.wait_recv()
+    arrived(qr.at[0], sq_in.at[pl.ds(0, 7)])
     lane = lax.broadcasted_iota(jnp.int32, (8, LANES), 1)
     mean_sq = jnp.zeros((8, LANES), F32)
     for m in range(MATS):
         mean_sq = mean_sq + jnp.where(lane == m, whole_sum(sq_in[2 * m]) / float(D * FF), 0.0)
     rms_out[...] = jnp.sqrt(mean_sq)
 
-    for q in range(2):
-        for s in STEPS:
-            first_copy(q, s).wait_send()
-            second_copy(q, s).wait_send()
-            third_copy(q, s).wait_send()
-        for n in range(4):
-            pair_copy(q, n).wait_send()
-    for dz, dc in COLUMN:
-        slot_copy(dz, dc).wait_send()
-    for copy in first + second + squares + spread:
-        copy.wait_send()
+    mom_pass.wait_send()
+    mom_sib.wait_send()
+    left(g1s.at[0], rs1)
+    left(g2s.at[0], rs2)
+    left(g3s.at[0], rs1)
+    left(g5s.at[0], full.at[0])
+    left(z2s.at[0], zout.at[pl.ds(0, 7)])
+    left(cs.at[0], column.at[pl.ds(0, 7)])
+    left(ps.at[0], plane.at[pl.ds(0, 15)])
+    left(ps2.at[0], plane2.at[pl.ds(0, 15)])
+    left(qs.at[0], sq_in.at[pl.ds(0, 7)])
     for dz in (0, 1, 3, 2):
         m = wrap(e + dz)
         if dz:
@@ -604,18 +612,20 @@
         out_specs=(ANY, VMEM, VMEM),
         scratch_shapes=[
             pltpu.VMEM(whole, BF16), pltpu.VMEM(whole, BF16),
-            pltpu.VMEM(large, BF16), pltpu.VMEM(large, BF16), pltpu.VMEM(large, BF16), pltpu.VMEM(large, BF16),
-            pltpu.VMEM(small, BF16), pltpu.VMEM(small, BF16), pltpu.VMEM(small, BF16),
+            pltpu.VMEM(large, BF16), pltpu.VMEM((CHUNKS, MATS, 2, SIDE, STRIP, HALF), BF16), pltpu.VMEM(large, BF16),
+            pltpu.VMEM(small, BF16), pltpu.VMEM((CHUNKS, MATS, 2, STRIP, HALF), BF16),
             pltpu.VMEM((MATS, BLOCK, HALF), BF16),
-            pltpu.VMEM((GROUPS, 2, BLOCK, HALF), BF16),
+            pltpu.VMEM((GROUPS * 2, BLOCK, HALF), BF16),
             pltpu.VMEM((GROUPS * SLOTS, BLOCK, HALF), BF16),
-            pltpu.VMEM((GROUPS, 2, BLOCK, HALF), BF16),
+            pltpu.VMEM((GROUPS * 2, BLOCK, HALF), BF16),
             pltpu.VMEM((SLOTS, GROUPS, ROWS, FF), F32),
             pltpu.VMEM((4, GROUPS, BLOCK, HALF), BF16), pltpu.VMEM((4, GROUPS, BLOCK, HALF), BF16),
             pltpu.VMEM((2, GROUPS, BLOCK, HALF), BF16),
+            pltpu.VMEM((GROUPS, 2, BLOCK, HALF), BF16),
+            pltpu.VMEM((GROUPS * BLOCK, HALF), BF16), pltpu.VMEM((GROUPS * BLOCK, HALF), BF16),
+            pltpu.VMEM((3, 32 * PART, LANES), F32),
             pltpu.VMEM((GROUPS, BLOCK, FF), F32),
             pltpu.VMEM((GROUPS, BLOCK, FF), BF16),
-            pltpu.VMEM((GROUPS * BLOCK, HALF), BF16),
             pltpu.VMEM((2, 2 * BLOCK, FF), BF16),
             pltpu.VMEM((32 * PART, LANES), BF16), pltpu.VMEM((2, 32 * PART, LANES), BF16),
             pltpu.VMEM((2, 3, 4 * PART, LANES), BF16),
@@ -626,13 +636,13 @@
             tile, tile, tile, tile,
             pltpu.VMEM((8, 8, LANES), F32), pltpu.VMEM((16, 8, LANES), F32), pltpu.VMEM((16, 8, LANES), F32),
             pltpu.VMEM((8, 8, LANES), F32),
-            DMA((CHUNKS, MATS)), DMA((CHUNKS, MATS)), DMA((CHUNKS, MATS)),
-            DMA((CHUNKS, MATS, 3)), DMA((CHUNKS, MATS, 3)), DMA((CHUNKS, MATS, 3)), DMA((CHUNKS, MATS, 3)),
-            DMA((CHUNKS, 8)), DMA((CHUNKS, 8)), DMA((CHUNKS,)), DMA((4,)), DMA((4,)), DMA((4,)), DMA((2,)),
-            DMA((7,)), DMA((7,)), DMA((15,)), DMA((15,)), DMA((3,)),
-            DMA((2, 3)), DMA((2, 3)), DMA((2, 3)), DMA((2, 3)), DMA((2, 3)), DMA((2, 3)),
-            DMA((2, 4)), DMA((2, 4)),
-            DMA((15,)), DMA((15,)), DMA((7,)), DMA((7,)), DMA((8,)), DMA((8,)), DMA((2, 2)), DMA((4,)), DMA((1,)),
+            DMA((CHUNKS,)), DMA((1,)), DMA((CHUNKS, MATS)),
+            DMA((3,)), DMA((CHUNKS,)), DMA((CHUNKS,)), DMA((3,)), DMA((CHUNKS,)), DMA((CHUNKS,)),
+            DMA((1,)), DMA((1,)), DMA((1,)), DMA((4,)), DMA((1,)), DMA((1,)), DMA((2,)),
+            DMA((1,)), DMA((1,)), DMA((1,)), DMA((1,)), DMA((3,)),
+            DMA((1,)), DMA((2,)), DMA((1,)), DMA((2,)), DMA((1,)), DMA((2, 3)), DMA((1,)), DMA((1,)),
+            DMA((1,)), DMA((1,)), DMA((1,)), DMA((1,)), DMA((1,)), DMA((1,)), DMA((1,)), DMA((2, 2)), DMA((4,)),
+            DMA((1,)),
         ],
         compiler_params=pltpu.CompilerParams(collective_id=0, has_side_effects=True, vmem_limit_bytes=60 << 20),
     )(owner_list, grad_terms.reshape(MATS, SIDE, SIDE, BLOCK, FF), momentum[0])

time: 112 us -> 105 us (0.938)
  Pallas kernels: 106 us -> 99.1 us
    pallas_call x1, Pallas kernels: 106 us -> 99.1 us  [per_device(): pl.pallas_call(muon_kernel, name='muon', out_shape=(jax.ShapeDtypeStruct(...]
where the time goes in v5:
time: 105 us
  Pallas kernels  99.1 us (94%)
  local copies, waits for them, and re-layouts  2.56 us (2%)
  other arithmetic  2.31 us (2%)
    pallas_call x1, Pallas kernels, per_device(): pl.pallas_call(muon_kernel, name='muon', out_shape=(jax.ShapeDtypeStruct(...  99.1 us
    convert_element_type x1, other arithmetic, per_device(): update = (scale_rms * rows).astype(BF16)  2.31 us

profile of v5, /device:TPU:1, one launch (start us, length us, event | category | flops | bytes accessed | tf_op | source)
XLA Modules:
  0.0 104.7 jit_solution(2816924211992050086)
XLA Ops:
  0.6 0.0 copy-start.1
  0.6 99.1 %muon.1 = (f32[2,4,56,1024]{3,2,1,0:T(8,128)}, bf16[4,56,1024]{2,1,0:T(8,128)(2,1)}, f32[8,128]{1,0:T(8,128)}) custom-call(s32[4]{0:T(128)} %owners.1, bf16[4,4,4,112,1024]{4,3,2,1,0:T(8,128)(2,1)} %bitcast.5, f32[2,4,56,1024]{3,2,1,0:T(8,128)} %bitcast.6), custom_call_target="tpu_custom_call" | custom-call | tf_op jit(solution)/shard_map/muon/pallas_call | solution.py:603
  99.8 0.0 copy-start
  99.8 1.3 %slice_bitcast_fusion = f32[4]{0:T(128)} fusion(f32[8,128]{1,0:T(8,128)} %get-tuple-element.9), kind=kLoop, calls=%fused_computation.4 | loop fusion | bytes 32 | tf_op jit(solution)/shard_map/squeeze | solution.py:654
  101.1 0.0 copy-done.1
  101.1 2.3 %fusion.1 = (bf16[4,56,1024]{2,1,0:T(8,128)(2,1)}, f32[4,56,1024]{2,1,0:T(8,128)}) fusion(bf16[4,56,1024]{2,1,0:T(8,128)(2,1)} %get-tuple-element.7, f32[4,56,1024]{2,1,0:T(8,128)S(1)} %copy-done.1), kind=kLoop, calls=%fused_computation.3 | loop fusion | flops 1376256 | bytes 2752512 | tf_op jit(solution)/shard_map/convert_element_type | solution.py:652
  103.4 0.0 copy-done
  103.4 1.2 %copy.9 = f32[1,2,4,56,1024]{4,3,2,1,0:T(8,128)} copy(f32[1,2,4,56,1024]{4,3,2,1,0:T(8,128)S(1)} %bitcast.7) | data formatting | bytes 3670016
Async XLA Ops:
  0.6 100.5 %copy-start.1 = (f32[4,56,1024]{2,1,0:T(8,128)S(1)}, f32[4,56,1024]{2,1,0:T(8,128)}, u32[]{:S(2)}) copy-start(f32[4,56,1024]{2,1,0:T(8,128)} %param.6) | copy-start | bytes 2752516
  99.8 3.7 %copy-start = (f32[2,4,56,1024]{3,2,1,0:T(8,128)S(1)}, f32[2,4,56,1024]{3,2,1,0:T(8,128)}, u32[]{:S(2)}) copy-start(f32[2,4,56,1024]{3,2,1,0:T(8,128)} %get-tuple-element.8) | copy-start | bytes 5505028

commit v6 on v5

--- a/solution.py
+++ b/solution.py
@@ -363,29 +363,28 @@
     factor = jnp.minimum(1.0, CLIP_RMS / jnp.sqrt(mean + MEAN_EPS))
 
 
-    def part4(ref, q, i):
-        return ref.at[pl.ds(pl.multiple_of((4 * q + i) * 4 * PART, 16), 4 * PART)]
+    def part(ref, q, i, b):
+        return ref.at[pl.ds(pl.multiple_of((8 * q + 2 * i + b) * 2 * PART, 16), 2 * PART)]
 
     def on(q, first, step):
         return (x, in_plane(step, 0)) if (q == 0) == first else (y, in_plane(0, step))
 
-    def first_copy(q, step):
+    def first_copy(q, step, b):
         pos, dev = on(q, True, step)
-        return remote(part4(packed, q, wrap(pos + step)), rs1.at[q, step - 1], g1s.at[0], g1r.at[q],
-                      dev)
-
-    def second_copy(q, step):
+        return remote(part(packed, q, wrap(pos + step), b), rs1.at[q, b, step - 1], g1s.at[0], g1r.at[q, b], dev)
+
+    def second_copy(q, step, b):
         _, dev = on(q, False, step)
-        return remote(midg.at[q], rs2.at[q, step - 1], g2s.at[0], g2r.at[q], dev)
-
-    def third_copy(q, step):
+        return remote(midg.at[q, b], rs2.at[q, b, step - 1], g2s.at[0], g2r.at[q, b], dev)
+
+    def third_copy(q, step, b):
         pos, dev = on(q, True, step)
-        ref = part4(full.at[c], q, pos)
-        return remote(ref, ref, g3s.at[0], g3r.at[q, step - 1], dev)
-
-    def pair_copy(q, n):
+        ref = part(full.at[c], q, pos, b)
+        return remote(ref, ref, g3s.at[0], g3r.at[q, b, step - 1], dev)
+
+    def pair_copy(q, n, b):
         pos, _ = on(q, True, 1)
-        ref = part4(full.at[c], q, wrap(pos + n))
+        ref = part(full.at[c], q, wrap(pos + n), b)
         return remote(ref, ref, g5s.at[0], g5r.at[0], in_column(0, 1))
 
     STEPS = (2, 1, 3)
@@ -400,7 +399,10 @@
 
         lax.fori_loop(0, 16, weigh, 0)
         for s in STEPS:
-            first_copy(q, s).start()
+            first_copy(q, s, 0).start()
+    for q in range(2):
+        for s in STEPS:
+            first_copy(q, s, 1).start()
 
     def direction(i, carry):
         for h in range(2):
@@ -438,28 +440,30 @@
         left(s2.at[which], tr2)
     left(zs.at[0], zin.at[pl.ds(0, 7)])
     left(m1s.at[0], mout.at[pl.ds(0, 3)])
-    for q in range(2):
-        arrived(g1r.at[q], rs1.at[q])
+    halves = [(q, b) for b in range(2) for q in range(2)]
+    for q, b in halves:
+        arrived(g1r.at[q, b], rs1.at[q, b])
         pos, _ = on(q, True, 1)
-        v = part4(packed, q, pos)[...].astype(F32) + rs1[q, 0].astype(F32)
-        midg[q] = (v + (rs1[q, 1].astype(F32) + rs1[q, 2].astype(F32))).astype(BF16)
+        v = part(packed, q, pos, b)[...].astype(F32) + rs1[q, b, 0].astype(F32)
+        midg[q, b] = (v + (rs1[q, b, 1].astype(F32) + rs1[q, b, 2].astype(F32))).astype(BF16)
         for s in STEPS:
-            second_copy(q, s).start()
-    for q in range(2):
-        arrived(g2r.at[q], rs2.at[q])
+            second_copy(q, s, b).start()
+    for q, b in halves:
+        arrived(g2r.at[q, b], rs2.at[q, b])
         pos, _ = on(q, True, 1)
-        v = midg[q].astype(F32) + rs2[q, 0].astype(F32)
-        part4(full.at[c], q, pos)[...] = (v + (rs2[q, 1].astype(F32) + rs2[q, 2].astype(F32))).astype(BF16)
+        v = midg[q, b].astype(F32) + rs2[q, b, 0].astype(F32)
+        part(full.at[c], q, pos, b)[...] = (v + (rs2[q, b, 1].astype(F32) + rs2[q, b, 2].astype(F32))).astype(BF16)
         for s in STEPS:
-            third_copy(q, s).start()
-        pair_copy(q, 0).start()
+            third_copy(q, s, b).start()
+        pair_copy(q, 0, b).start()
     acc4[...] = total_of(pr2, plane2, 16)
     spread_column(acc4, sq_in, qs, qr)
     inv = 1.0 / (jnp.sqrt(whole_sum(acc4[...])) + NORM_EPS)
-    for s in (1, 3, 2):
-        for q in range(2):
-            third_copy(q, s).wait_recv()
-            pair_copy(q, 4 - s).start()
+    for b in range(2):
+        for s in (1, 3, 2):
+            for q in range(2):
+                third_copy(q, s, b).wait_recv()
+                pair_copy(q, 4 - s, b).start()
     arrived(g5r.at[0], full.at[other])
     for k in range(2):
         at = 0
@@ -628,9 +632,9 @@
             pltpu.VMEM((GROUPS, BLOCK, FF), BF16),
             pltpu.VMEM((2, 2 * BLOCK, FF), BF16),
             pltpu.VMEM((32 * PART, LANES), BF16), pltpu.VMEM((2, 32 * PART, LANES), BF16),
-            pltpu.VMEM((2, 3, 4 * PART, LANES), BF16),
-            pltpu.VMEM((2, 4 * PART, LANES), BF16),
-            pltpu.VMEM((2, 3, 4 * PART, LANES), BF16),
+            pltpu.VMEM((2, 2, 3, 2 * PART, LANES), BF16),
+            pltpu.VMEM((2, 2, 2 * PART, LANES), BF16),
+            pltpu.VMEM((2, 2, 3, 2 * PART, LANES), BF16),
             square, square, square, square,
             pltpu.VMEM((2, 2, BLOCK, HALF), BF16), pltpu.VMEM((MATS, BLOCK, HALF), BF16),
             tile, tile, tile, tile,
@@ -640,7 +644,7 @@
             DMA((3,)), DMA((CHUNKS,)), DMA((CHUNKS,)), DMA((3,)), DMA((CHUNKS,)), DMA((CHUNKS,)),
             DMA((1,)), DMA((1,)), DMA((1,)), DMA((4,)), DMA((1,)), DMA((1,)), DMA((2,)),
             DMA((1,)), DMA((1,)), DMA((1,)), DMA((1,)), DMA((3,)),
-            DMA((1,)), DMA((2,)), DMA((1,)), DMA((2,)), DMA((1,)), DMA((2, 3)), DMA((1,)), DMA((1,)),
+            DMA((1,)), DMA((2, 2)), DMA((1,)), DMA((2, 2)), DMA((1,)), DMA((2, 2, 3)), DMA((1,)), DMA((1,)),
             DMA((1,)), DMA((1,)), DMA((1,)), DMA((1,)), DMA((1,)), DMA((1,)), DMA((1,)), DMA((2, 2)), DMA((4,)),
             DMA((1,)),
         ],

time: 105 us -> 104 us (level)
  no operation moved by 1% of the time
where the time goes in v6:
time: 104 us
  Pallas kernels  98.4 us (95%)
  local copies, waits for them, and re-layouts  2.56 us (2%)
  other arithmetic  2.31 us (2%)
    pallas_call x1, Pallas kernels, per_device(): pl.pallas_call(muon_kernel, name='muon', out_shape=(jax.ShapeDtypeStruct(...  98.4 us
    convert_element_type x1, other arithmetic, per_device(): update = (scale_rms * rows).astype(BF16)  2.31 us

profile of v6, /device:TPU:1, one launch (start us, length us, event | category | flops | bytes accessed | tf_op | source)
XLA Modules:
  0.0 103.9 jit_solution(3349917159933215178)
XLA Ops:
  0.6 0.0 copy-start.1
  0.6 98.4 %muon.1 = (f32[2,4,56,1024]{3,2,1,0:T(8,128)}, bf16[4,56,1024]{2,1,0:T(8,128)(2,1)}, f32[8,128]{1,0:T(8,128)}) custom-call(s32[4]{0:T(128)} %owners.1, bf16[4,4,4,112,1024]{4,3,2,1,0:T(8,128)(2,1)} %bitcast.5, f32[2,4,56,1024]{3,2,1,0:T(8,128)} %bitcast.6), custom_call_target="tpu_custom_call" | custom-call | tf_op jit(solution)/shard_map/muon/pallas_call | solution.py:607
  99.1 0.0 copy-start
  99.1 1.3 %slice_bitcast_fusion = f32[4]{0:T(128)} fusion(f32[8,128]{1,0:T(8,128)} %get-tuple-element.9), kind=kLoop, calls=%fused_computation.4 | loop fusion | bytes 32 | tf_op jit(solution)/shard_map/squeeze | solution.py:658
  100.4 0.0 copy-done.1
  100.4 2.3 %fusion.1 = (bf16[4,56,1024]{2,1,0:T(8,128)(2,1)}, f32[4,56,1024]{2,1,0:T(8,128)}) fusion(bf16[4,56,1024]{2,1,0:T(8,128)(2,1)} %get-tuple-element.7, f32[4,56,1024]{2,1,0:T(8,128)S(1)} %copy-done.1), kind=kLoop, calls=%fused_computation.3 | loop fusion | flops 1376256 | bytes 2752512 | tf_op jit(solution)/shard_map/convert_element_type | solution.py:656
  102.7 0.0 copy-done
  102.7 1.2 %copy.9 = f32[1,2,4,56,1024]{4,3,2,1,0:T(8,128)} copy(f32[1,2,4,56,1024]{4,3,2,1,0:T(8,128)S(1)} %bitcast.7) | data formatting | bytes 3670016
Async XLA Ops:
  0.6 99.8 %copy-start.1 = (f32[4,56,1024]{2,1,0:T(8,128)S(1)}, f32[4,56,1024]{2,1,0:T(8,128)}, u32[]{:S(2)}) copy-start(f32[4,56,1024]{2,1,0:T(8,128)} %param.6) | copy-start | bytes 2752516
  99.1 3.7 %copy-start = (f32[2,4,56,1024]{3,2,1,0:T(8,128)S(1)}, f32[2,4,56,1024]{3,2,1,0:T(8,128)}, u32[]{:S(2)}) copy-start(f32[2,4,56,1024]{3,2,1,0:T(8,128)} %get-tuple-element.8) | copy-start | bytes 5505028

commit v7 on v6

--- a/solution.py
+++ b/solution.py
@@ -553,7 +553,7 @@
     mean_sq = jnp.zeros((8, LANES), F32)
     for m in range(MATS):
         mean_sq = mean_sq + jnp.where(lane == m, whole_sum(sq_in[2 * m]) / float(D * FF), 0.0)
-    rms_out[...] = jnp.sqrt(mean_sq)
+    rms_out[...] = jnp.sqrt(mean_sq)[:1, :MATS]
 
     mom_pass.wait_send()
     mom_sib.wait_send()
@@ -610,7 +610,7 @@
         out_shape=(
             jax.ShapeDtypeStruct((SLOTS, GROUPS, ROWS, FF), F32),
             jax.ShapeDtypeStruct((MATS, ROWS, FF), BF16),
-            jax.ShapeDtypeStruct((8, LANES), F32),
+            jax.ShapeDtypeStruct((1, MATS), F32),
         ),
         in_specs=[SMEM, ANY, ANY],
         out_specs=(ANY, VMEM, VMEM),
@@ -655,7 +655,7 @@
     scale_rms = 0.2 * math.sqrt(max(D, FF))
     update = (scale_rms * rows).astype(BF16)
     new_weights = weights * (1.0 - LEARN * DECAY) - LEARN * scale_rms * rows
-    return (new_weights, update, new_mom[None], rms[0, :MATS])
+    return (new_weights, update, new_mom[None], rms.reshape(MATS))
 
 
 def solution(mesh):

time: 104 us -> 103 us (level)
    squeeze x1 -> x0, local copies, waits for them, and re-layouts: 1.33 us -> none  [per_device(): return (new_weights, update, new_mom[None], rms[0, :MATS])]
where the time goes in v7:
time: 103 us
  Pallas kernels  98.4 us (96%)
  other arithmetic  2.44 us (2%)
  local copies, waits for them, and re-layouts  1.75 us (2%)
    pallas_call x1, Pallas kernels, per_device(): pl.pallas_call(muon_kernel, name='muon', out_shape=(jax.ShapeDtypeStruct(...  98.4 us
    convert_element_type x1, other arithmetic, per_device(): update = (scale_rms * rows).astype(BF16)  2.44 us

profile of v7, /device:TPU:1, one launch (start us, length us, event | category | flops | bytes accessed | tf_op | source)
XLA Modules:
  0.0 103.3 jit_solution(2614955375150863290)
XLA Ops:
  0.6 0.0 copy-start.1
  0.6 98.4 %muon.1 = (f32[2,4,56,1024]{3,2,1,0:T(8,128)}, bf16[4,56,1024]{2,1,0:T(8,128)(2,1)}, f32[1,4]{1,0:T(1,128)}) custom-call(s32[4]{0:T(128)} %owners.1, bf16[4,4,4,112,1024]{4,3,2,1,0:T(8,128)(2,1)} %bitcast.4, f32[2,4,56,1024]{3,2,1,0:T(8,128)} %bitcast.5), custom_call_target="tpu_custom_call" | custom-call | tf_op jit(solution)/shard_map/muon/pallas_call | solution.py:607
  99.1 0.0 copy-start
  99.1 0.0 copy-done.1
  99.1 2.4 %fusion.1 = (bf16[4,56,1024]{2,1,0:T(8,128)(2,1)}, f32[4,56,1024]{2,1,0:T(8,128)}) fusion(bf16[4,56,1024]{2,1,0:T(8,128)(2,1)} %get-tuple-element.7, f32[4,56,1024]{2,1,0:T(8,128)S(1)} %copy-done.1), kind=kLoop, calls=%fused_computation.3 | loop fusion | flops 1376256 | bytes 2752512 | tf_op jit(solution)/shard_map/convert_element_type | solution.py:656
  101.5 0.0 copy-done
  101.5 0.0 copy-start.2
  101.5 1.2 %copy.10 = f32[1,2,4,56,1024]{4,3,2,1,0:T(8,128)} copy(f32[1,2,4,56,1024]{4,3,2,1,0:T(8,128)S(1)} %bitcast.6) | data formatting | bytes 3670016
  102.8 0.0 copy-done.2
  102.8 0.5 copy.11
Async XLA Ops:
  0.6 98.5 %copy-start.1 = (f32[4,56,1024]{2,1,0:T(8,128)S(1)}, f32[4,56,1024]{2,1,0:T(8,128)}, u32[]{:S(2)}) copy-start(f32[4,56,1024]{2,1,0:T(8,128)} %param.6) | copy-start | bytes 2752516
  99.1 2.5 %copy-start = (f32[2,4,56,1024]{3,2,1,0:T(8,128)S(1)}, f32[2,4,56,1024]{3,2,1,0:T(8,128)}, u32[]{:S(2)}) copy-start(f32[2,4,56,1024]{3,2,1,0:T(8,128)} %get-tuple-element.8) | copy-start | bytes 5505028
  101.5 1.2 %copy-start.2 = (f32[1,4]{1,0:T(1,128)S(1)}, f32[1,4]{1,0:T(1,128)}, u32[]{:S(2)}) copy-start(f32[1,4]{1,0:T(1,128)} %get-tuple-element.9) | copy-start | bytes 52

commit v8 on v7

--- a/solution.py
+++ b/solution.py
@@ -326,11 +326,7 @@
 
     spread_column(acc, column, cs, cr)
     send_strips(LAST)
-    acc2[...] = total_of(cr, column, 8)
-    spread_plane(acc2, plane, ps, pr)
     mom_pass.wait_recv()
-    arrived(zr.at[0], zin.at[pl.ds(0, 7)])
-    pltpu.make_async_copy(zin.at[0], zin.at[0], zl.at[0]).wait()
 
     def unpack(i, carry):
         parts = [mall[k, i].astype(F32) for k in range(2)]
@@ -342,11 +338,27 @@
     lax.fori_loop(0, GROUPS, unpack, 0)
     for j in range(4):
         cols = pl.ds(pl.multiple_of((2 * (j % 2) + c) * LANES, LANES), LANES)
-        gright[:, j * LANES:(j + 1) * LANES] = jnp.concatenate([zin[2 * n + j // 2, :, cols] for n in range(GROUPS)], axis=0)
         mright[:, j * LANES:(j + 1) * LANES] = Mb[:, j // 2, :, cols].reshape(GROUPS * BLOCK, LANES)
 
     def outer(left, right):
         return lax.dot_general(left, right, (((0,), (0,)), ((), ())), preferred_element_type=F32)
+
+    at = 0
+    for i in range(4):
+        cols = slice((i % 2) * PANEL, (i % 2 + 1) * PANEL)
+        mm = outer(Mb[:, i // 2, :, cols].reshape(GROUPS * BLOCK, PANEL), mright[:, i * LANES:])
+        for j in range(4 - i):
+            grams[2, at:at + PANEL] = mm[:, j * LANES:(j + 1) * LANES]
+            at += PANEL
+
+    acc2[...] = total_of(cr, column, 8)
+    spread_plane(acc2, plane, ps, pr)
+    arrived(zr.at[0], zin.at[pl.ds(0, 7)])
+    pltpu.make_async_copy(zin.at[0], zin.at[0], zl.at[0]).wait()
+
+    for j in range(4):
+        cols = pl.ds(pl.multiple_of((2 * (j % 2) + c) * LANES, LANES), LANES)
+        gright[:, j * LANES:(j + 1) * LANES] = jnp.concatenate([zin[2 * n + j // 2, :, cols] for n in range(GROUPS)], axis=0)
 
     at = 0
     for i in range(4):
@@ -354,9 +366,9 @@
         gleft = jnp.concatenate([zin[2 * n + i // 2, :, cols] for n in range(GROUPS)], axis=0)
         mleft = Mb[:, i // 2, :, cols].reshape(GROUPS * BLOCK, PANEL)
         gr, mr = gright[:, i * LANES:], mright[:, i * LANES:]
-        gg, gm, mm = outer(gleft, gr), outer(gleft, mr) + outer(mleft, gr), outer(mleft, mr)
+        gg, gm = outer(gleft, gr), outer(gleft, mr) + outer(mleft, gr)
         for j in range(4 - i):
-            for n, v in enumerate((gg, gm, mm)):
+            for n, v in enumerate((gg, gm)):
                 grams[n, at:at + PANEL] = v[:, j * LANES:(j + 1) * LANES]
             at += PANEL
     mean = whole_sum(total_of(pr, plane, 16)) / float(MATS * D * FF)

time: 103 us -> 103 us (level)
  no operation moved by 1% of the time
where the time goes in v8:
time: 103 us
  Pallas kernels  98.4 us (96%)
  other arithmetic  2.44 us (2%)
  local copies, waits for them, and re-layouts  1.75 us (2%)
    pallas_call x1, Pallas kernels, per_device(): pl.pallas_call(muon_kernel, name='muon', out_shape=(jax.ShapeDtypeStruct(...  98.4 us
    convert_element_type x1, other arithmetic, per_device(): update = (scale_rms * rows).astype(BF16)  2.44 us

profile of v8, /device:TPU:1, one launch (start us, length us, event | category | flops | bytes accessed | tf_op | source)
XLA Modules:
  0.0 103.3 jit_solution(15914305341586223150)
XLA Ops:
  0.6 0.0 copy-start.1
  0.6 98.4 %muon.1 = (f32[2,4,56,1024]{3,2,1,0:T(8,128)}, bf16[4,56,1024]{2,1,0:T(8,128)(2,1)}, f32[1,4]{1,0:T(1,128)}) custom-call(s32[4]{0:T(128)} %owners.1, bf16[4,4,4,112,1024]{4,3,2,1,0:T(8,128)(2,1)} %bitcast.4, f32[2,4,56,1024]{3,2,1,0:T(8,128)} %bitcast.5), custom_call_target="tpu_custom_call" | custom-call | tf_op jit(solution)/shard_map/muon/pallas_call | solution.py:619
  99.1 0.0 copy-start
  99.1 0.0 copy-done.1
  99.1 2.4 %fusion.1 = (bf16[4,56,1024]{2,1,0:T(8,128)(2,1)}, f32[4,56,1024]{2,1,0:T(8,128)}) fusion(bf16[4,56,1024]{2,1,0:T(8,128)(2,1)} %get-tuple-element.7, f32[4,56,1024]{2,1,0:T(8,128)S(1)} %copy-done.1), kind=kLoop, calls=%fused_computation.3 | loop fusion | flops 1376256 | bytes 2752512 | tf_op jit(solution)/shard_map/convert_element_type | solution.py:668
  101.5 0.0 copy-done
  101.5 0.0 copy-start.2
  101.5 1.2 %copy.10 = f32[1,2,4,56,1024]{4,3,2,1,0:T(8,128)} copy(f32[1,2,4,56,1024]{4,3,2,1,0:T(8,128)S(1)} %bitcast.6) | data formatting | bytes 3670016
  102.8 0.0 copy-done.2
  102.8 0.5 copy.11
Async XLA Ops:
  0.6 98.5 %copy-start.1 = (f32[4,56,1024]{2,1,0:T(8,128)S(1)}, f32[4,56,1024]{2,1,0:T(8,128)}, u32[]{:S(2)}) copy-start(f32[4,56,1024]{2,1,0:T(8,128)} %param.6) | copy-start | bytes 2752516
  99.1 2.5 %copy-start = (f32[2,4,56,1024]{3,2,1,0:T(8,128)S(1)}, f32[2,4,56,1024]{3,2,1,0:T(8,128)}, u32[]{:S(2)}) copy-start(f32[2,4,56,1024]{3,2,1,0:T(8,128)} %get-tuple-element.8) | copy-start | bytes 5505028
  101.5 1.2 %copy-start.2 = (f32[1,4]{1,0:T(1,128)S(1)}, f32[1,4]{1,0:T(1,128)}, u32[]{:S(2)}) copy-start(f32[1,4]{1,0:T(1,128)} %get-tuple-element.9) | copy-start | bytes 52
